TPU v7x, 32 devices: a whole 2x2x4 slice. The times are simulated.
32 devices in a mesh: dp: 2 (over core), row: 4 (over z), col: 4 (over y, x).
Axes of the slice: x: 2, y: 2, z: 4, core: 2. Of those that a mesh axis runs over, the one named last changes fastest.
Arguments:
- tokens: bfloat16 [1024, 8192], P('col', ('dp', 'row')), may hold values from -6.5 to 6.5
- w_qkv: bfloat16 [1024, 3, 1024], P('col', None, 'row'), may hold values from -0.1875 to 0.1875
- b_qv: bfloat16 [2, 1024], P(None, 'row'), may hold values from -0.59765625 to 0.59765625
- w_out: bfloat16 [1024, 1024], P('row', 'col'), may hold values from -1.5 to 1.5
- b_out: bfloat16 [1024], P('col'), may hold values from -2 to 2
- norm1_gain: bfloat16 [1024], P('col'), may hold values from 0.25 to 1.75
- norm1_shift: bfloat16 [1024], P('col'), may hold values from -2 to 2
- w_up: bfloat16 [1024, 4096], P('col', 'row'), may hold values from -0.1875 to 0.1875
- b_up: bfloat16 [4096], P('row'), may hold values from -3 to 3
- w_down: bfloat16 [4096, 1024], P('row', 'col'), may hold values from -0.09375 to 0.09375
- b_down: bfloat16 [1024], P('col'), may hold values from -2 to 2
- norm2_gain: bfloat16 [1024], P('col'), may hold values from 0.25 to 1.75
- norm2_shift: bfloat16 [1024], P('col'), may hold values from -2 to 2
- cotangent: bfloat16 [1024, 8192], P('col', ('dp', 'row')), may hold values from -6 to 6
Outputs:
- out: bfloat16 [1024, 8192], P('col', ('dp', 'row'))
- grad_tokens: float32 [1024, 8192], P('col', ('dp', 'row'))
- grad_w_qkv: float32 [1024, 3, 1024], P('col', None, 'row')
- grad_b_qv: float32 [2, 1024], P(None, 'row')
- grad_w_out: float32 [1024, 1024], P('row', 'col')
- grad_b_out: float32 [1024], P('col')
- grad_norm1_gain: float32 [1024], P('col')
- grad_norm1_shift: float32 [1024], P('col')
- grad_w_up: float32 [1024, 4096], P('col', 'row')
- grad_b_up: float32 [4096], P('row')
- grad_w_down: float32 [4096, 1024], P('row', 'col')
- grad_b_down: float32 [1024], P('col')
- grad_norm2_gain: float32 [1024], P('col')
- grad_norm2_shift: float32 [1024], P('col')
All inputs are finite; a program needn't handle non-finite values.
Results may differ from a plain program's by a relative error of at most 0.014.
Values may be sent and summed in bfloat16 or wider, within the bound.
No kernel may reach another device: no remote copies, remote signals or barrier semaphores. Data moves between devices by JAX's collectives and lax.ppermute only.
A program may use at most 256 MiB of HBM per device.

v0:
```python
import jax
import jax.numpy as jnp
from jax import lax
from jax.experimental import pallas as pl
from jax.experimental.pallas import tpu as pltpu
from jax.sharding import Mesh
from jax.sharding import PartitionSpec as P

D = 1024
HEAD_DIM = 64
SEQ = 1024


norm_eps = 1e-05


def matmul(first_mat, second_mat):
    return jnp.dot(first_mat, second_mat, preferred_element_type=jnp.float32)


def against(first_mat, second_mat):
    return lax.dot_general(
        first_mat, second_mat, (((1,), (1,)), ((), ())), preferred_element_type=jnp.float32
    )


def inner_rows(first_mat, second_mat):
    return lax.dot_general(
        first_mat, second_mat, (((0,), (0,)), ((), ())), preferred_element_type=jnp.float32
    )


def by_row(values):
    return lax.all_gather(values, "row", axis=0, tiled=True)


def by_col(values):
    return lax.all_gather(values, "col", axis=0, tiled=True)


def reduce_col(source, weight, transposed):
    row_count = source.shape[0] // lax.axis_size("col")

    def partial_value(row_start, row_num):
        return against(source, weight) if transposed else matmul(source, weight)

    return lax.psum_scatter(
        partial_value(jnp.int32(0), row_count * lax.axis_size("col")),
        "col",
        scatter_dimension=0,
        tiled=True,
    )


def reduce_row(source, weight, transposed):
    row_count = source.shape[0] // lax.axis_size("row")

    def partial_value(row_start, row_num):
        return against(source, weight) if transposed else matmul(source, weight)

    return lax.psum_scatter(
        partial_value(jnp.int32(0), row_count * lax.axis_size("row")),
        "row",
        scatter_dimension=0,
        tiled=True,
    )


def feature_totals(first_terms, second_terms):
    return lax.psum((jnp.sum(first_terms, axis=1), jnp.sum(second_terms, axis=1)), "col")


def norm_forward(residual, gain_vec, shift_vec):
    totals = feature_totals(residual, residual * residual)
    mean_rows = totals[0][:, None] / D
    spread = totals[1][:, None] / D - mean_rows * mean_rows
    scale_rows = lax.rsqrt(spread + norm_eps)
    normed = (residual - mean_rows) * scale_rows
    return (normed * gain_vec + shift_vec, normed, scale_rows)


def norm_backward(grad_in, normed, scale_rows, gain_vec):
    scaled = grad_in * gain_vec
    totals = feature_totals(scaled, scaled * normed)
    grad_resid = scale_rows * (scaled - totals[0][:, None] / D - normed * (totals[1][:, None] / D))
    return (grad_resid, jnp.sum(grad_in * normed, axis=0), jnp.sum(grad_in, axis=0))


def gelu_exact(values):
    return jax.nn.gelu(values, approximate=False)


def by_heads(values, head_count):
    seq_count = values.shape[0] // SEQ
    return values.reshape(seq_count, SEQ, head_count, HEAD_DIM)


def attention_forward(queries, key_seq, value_seq):
    block_len = min(512, SEQ)
    outputs = []
    log_parts = []
    for offset in range(0, SEQ, block_len):
        query_block = queries[:, offset : offset + block_len]
        scores = jnp.einsum(
            "nqhd,nkhd->nhqk", query_block, key_seq, preferred_element_type=jnp.float32
        )
        row_max = jnp.max(scores, axis=-1, keepdims=True)
        exp_scores = jnp.exp(scores - row_max)
        denom = jnp.sum(exp_scores, axis=-1, keepdims=True)
        probs_low = (exp_scores / denom).astype(jnp.bfloat16)
        outputs.append(
            jnp.einsum("nhqk,nkhd->nqhd", probs_low, value_seq, preferred_element_type=jnp.float32)
        )
        log_parts.append(row_max + jnp.log(denom))
    attended = jnp.concatenate(outputs, axis=1)
    rows_here = attended.shape[0] * SEQ
    return (
        attended.reshape(rows_here, -1).astype(jnp.bfloat16),
        jnp.concatenate(log_parts, axis=2),
    )


def attention_backward(queries, key_seq, value_seq, grad_seq, log_norm):
    block_len = min(512, SEQ)
    grad_query_parts = []
    grad_key = jnp.zeros(key_seq.shape, jnp.float32)
    grad_value = jnp.zeros(value_seq.shape, jnp.float32)
    for offset in range(0, SEQ, block_len):
        query_block = queries[:, offset : offset + block_len]
        grad_block = grad_seq[:, offset : offset + block_len]
        scores = jnp.einsum(
            "nqhd,nkhd->nhqk", query_block, key_seq, preferred_element_type=jnp.float32
        )
        probs = jnp.exp(scores - log_norm[:, :, offset : offset + block_len])
        grad_probs = jnp.einsum(
            "nqhd,nkhd->nhqk", grad_block, value_seq, preferred_element_type=jnp.float32
        )
        row_delta = jnp.sum(grad_probs * probs, axis=-1, keepdims=True)
        grad_scores = (probs * (grad_probs - row_delta)).astype(jnp.bfloat16)
        grad_query_parts.append(
            jnp.einsum("nhqk,nkhd->nqhd", grad_scores, key_seq, preferred_element_type=jnp.float32)
        )
        grad_key = grad_key + jnp.einsum(
            "nhqk,nqhd->nkhd", grad_scores, query_block, preferred_element_type=jnp.float32
        )
        grad_value = grad_value + jnp.einsum(
            "nhqk,nqhd->nkhd",
            probs.astype(jnp.bfloat16),
            grad_block,
            preferred_element_type=jnp.float32,
        )
    grad_query = jnp.concatenate(grad_query_parts, axis=1)
    rows_here = grad_query.shape[0] * SEQ
    return (
        grad_query.reshape(rows_here, -1).astype(jnp.bfloat16),
        grad_key.reshape(rows_here, -1).astype(jnp.bfloat16),
        grad_value.reshape(rows_here, -1).astype(jnp.bfloat16),
    )


def shards(
    tokens,
    w_qkv,
    b_qv,
    w_out,
    b_out,
    norm1_gain,
    norm1_shift,
    w_up,
    b_up,
    w_down,
    b_down,
    norm2_gain,
    norm2_shift,
    cotangent,
):
    token_major = tokens.T
    width_col = token_major.shape[1]
    width_row = w_out.shape[0]
    qkv_weight = w_qkv.reshape(width_col, 3 * width_row)
    query_scale = HEAD_DIM ** (-0.5)
    head_count = width_row // HEAD_DIM
    gathered_in = by_row(token_major)
    projected = reduce_col(gathered_in, qkv_weight, False).reshape(-1, 3, width_row)
    queries = ((projected[:, 0] + b_qv[0]) * query_scale).astype(jnp.bfloat16)
    key_rows = projected[:, 1].astype(jnp.bfloat16)
    value_rows = (projected[:, 2] + b_qv[1]).astype(jnp.bfloat16)
    query_seq = by_heads(queries, head_count)
    key_seq = by_heads(key_rows, head_count)
    value_seq = by_heads(value_rows, head_count)
    attended, log_norm = attention_forward(query_seq, key_seq, value_seq)
    gathered_att = by_col(attended)
    attn_out = reduce_row(gathered_att, w_out, False) + b_out
    residual1 = token_major.astype(jnp.float32) + attn_out
    normed_a, normed1, scale1 = norm_forward(residual1, norm1_gain, norm1_shift)
    low_a = normed_a.astype(jnp.bfloat16)
    gathered_a = by_row(low_a)
    pre_act = reduce_col(gathered_a, w_up, False) + b_up
    hidden, gelu_pull = jax.vjp(gelu_exact, pre_act)
    hidden_low = hidden.astype(jnp.bfloat16)
    gathered_h = by_col(hidden_low)
    branch_out = reduce_row(gathered_h, w_down, False)
    residual2 = normed_a + branch_out + b_down
    result, normed2, scale2 = norm_forward(residual2, norm2_gain, norm2_shift)
    grad_out = cotangent.T.astype(jnp.float32)
    grad_r2, gain2_part, shift2_part = norm_backward(grad_out, normed2, scale2, norm2_gain)
    down_bias_part = jnp.sum(grad_r2, axis=0)
    grad_branch = grad_r2.astype(jnp.bfloat16)
    gathered_df = by_row(grad_branch)
    down_grad = inner_rows(gathered_h, gathered_df)
    grad_hidden = reduce_col(gathered_df, w_down, True)
    grad_pre = gelu_pull(grad_hidden)[0].astype(jnp.bfloat16)
    gathered_dz = by_col(grad_pre)
    up_grad = inner_rows(gathered_a, gathered_dz)
    up_bias_grad = jnp.sum(gathered_dz, axis=0, dtype=jnp.float32)
    grad_a_ff = reduce_row(gathered_dz, w_up, True)
    grad_a = grad_r2 + grad_a_ff
    grad_r1, gain1_part, shift1_part = norm_backward(grad_a, normed1, scale1, norm1_gain)
    out_bias_part = jnp.sum(grad_r1, axis=0)
    gathered_datt = by_row(grad_r1.astype(jnp.bfloat16))
    out_grad = inner_rows(gathered_att, gathered_datt)
    grad_attended = reduce_col(gathered_datt, w_out, True).astype(jnp.bfloat16)
    grad_seq = by_heads(grad_attended, head_count)
    grad_query, grad_key, grad_value = attention_backward(
        query_seq, key_seq, value_seq, grad_seq, log_norm
    )
    grad_proj = jnp.stack([grad_query * query_scale, grad_key, grad_value], axis=1).reshape(
        -1, 3 * width_row
    )
    gathered_dqkv = by_col(grad_proj)
    qkv_grad = inner_rows(gathered_in, gathered_dqkv).reshape(width_col, 3, width_row)
    bias_rows = jnp.sum(gathered_dqkv, axis=0, dtype=jnp.float32).reshape(3, width_row)
    qv_bias_grad = jnp.stack([bias_rows[0], bias_rows[2]])
    grad_input = reduce_row(gathered_dqkv, qkv_weight, True) + grad_r1
    norm_sums = lax.psum(
        (gain1_part, shift1_part, gain2_part, shift2_part, out_bias_part, down_bias_part),
        ("dp", "row"),
    )
    weight_sums = lax.psum(
        (qkv_grad, qv_bias_grad, out_grad, up_grad, up_bias_grad, down_grad), "dp"
    )
    return (
        result.astype(jnp.bfloat16).T,
        grad_input.T,
        weight_sums[0],
        weight_sums[1],
        weight_sums[2],
        norm_sums[4],
        norm_sums[0],
        norm_sums[1],
        weight_sums[3],
        weight_sums[4],
        weight_sums[5],
        norm_sums[5],
        norm_sums[2],
        norm_sums[3],
    )


BF = jnp.bfloat16
F32 = jnp.float32
PAIR = ((0, 1), (1, 0))
MEBIBYTE = 1024 * 1024
BLOCK = 256


def flip(values, axis_name):
    return lax.ppermute(values, axis_name, PAIR)


def shift(values, axis_name, step):
    size = lax.axis_size(axis_name)
    return lax.ppermute(values, axis_name, [(i, (i + step) % size) for i in range(size)])


def in_order(index, mine, other, axis):
    first = jnp.where(index == 0, mine, other)
    second = jnp.where(index == 0, other, mine)
    return jnp.concatenate([first, second], axis)


def four_in_order(low_bit, high_bit, parts, axis):
    low = [jnp.where(low_bit == 0, parts[i], parts[i ^ 1]) for i in range(4)]
    full = [jnp.where(high_bit == 0, low[i], low[i ^ 2]) for i in range(4)]
    return jnp.concatenate(full, axis)


def cut(values, index, size, axis):
    return lax.dynamic_slice_in_dim(values, index * size, size, axis)


def after(values, *earlier):
    return lax.optimization_barrier((values, earlier))[0]


def part(index, size):
    return pl.ds(pl.multiple_of(index * size, size), size)


def kernel_call(kernel, name, outs, places, *inputs, grid=1, specs=None, out_specs=None, scratch=(), vmem=16, long=False):
    return pl.pallas_call(
        kernel,
        grid_spec=pltpu.PrefetchScalarGridSpec(
            num_scalar_prefetch=1,
            grid=(grid,),
            in_specs=[fixed(x.shape) for x in inputs] if specs is None else specs,
            out_specs=[fixed(shape) for shape, _ in outs] if out_specs is None else out_specs,
            scratch_shapes=list(scratch),
        ),
        out_shape=[jax.ShapeDtypeStruct(shape, dtype) for shape, dtype in outs],
        compiler_params=pltpu.CompilerParams(vmem_limit_bytes=vmem * MEBIBYTE),
        cost_estimate=pl.CostEstimate(
            flops=10**10 if long else 1, bytes_accessed=10**8 if long else 1, transcendentals=0
        ),
        name=name,
    )(places, *inputs)


def fixed(shape):
    return pl.BlockSpec(shape, lambda step, places: (0,) * len(shape))


def stepped(shape, axis):
    return pl.BlockSpec(
        shape, lambda step, places: tuple(step if i == axis else 0 for i in range(len(shape)))
    )


def prepare_attn_kernel(places, w_qkv, b_qv, w_out, *refs):
    vectors, (keep, send, turned) = refs[:-3], refs[-3:]
    head = turned.shape[1] // 4
    for piece in range(3):
        turned[piece] = w_qkv[piece].T
    for ref, quarter in ((keep, places[0]), (send, places[1])):
        for piece in range(3):
            ref[piece * head : (piece + 1) * head] = turned[piece, part(quarter, head), :]
        bias = b_qv[...].astype(F32)
        own = sum(
            jnp.where(quarter == q, bias[:, q * head : (q + 1) * head], 0.0) for q in range(4)
        )
        line = jnp.concatenate([own[0:1], own[1:2]], 1)
        line = jnp.concatenate([line, jnp.zeros((1, keep.shape[1] - 2 * head), F32)], 1)
        rows = [jnp.broadcast_to(line, (8, keep.shape[1]))]
        rows += [vector[...].astype(F32).reshape(1, -1) for vector in vectors]
        rows += [jnp.zeros((2, keep.shape[1]), F32)]
        ref[3 * head : 3 * head + 16] = jnp.concatenate(rows, 0).astype(BF)
        ref[3 * head + 16 :] = w_out[part(quarter, head), :]


def prepare_ff_kernel(places, w_up, w_down, keep, send):
    for ref, quarter in ((keep, places[0]), (send, places[1])):
        ref[:BLOCK] = w_up[:, part(quarter, BLOCK)].T
        ref[BLOCK:] = w_down[part(quarter, BLOCK), :]


def attend_kernel(places, x00, x01, x10, x11, own, far, qkv_ref, out_ref, norm_ref, *weight_refs):
    head_rows = qkv_ref.shape[2]
    total = None
    for side, pair in ((0, (x00, x01)), (1, (x10, x11))):
        mine = (places[3] ^ side) == places[2]
        for end, x in enumerate(pair):
            weight = jnp.where(mine, own[0, end, : 3 * head_rows], far[0, end, : 3 * head_rows])
            weight_refs[2 * side + end][0] = weight
            piece = matmul(weight, x[...])
            total = piece if total is None else total + piece
    bias = own[0, 0, 3 * head_rows : 3 * head_rows + 8].astype(F32)[0:1, : 2 * head_rows]
    bias = jnp.broadcast_to(bias, (2 * head_rows, 2 * head_rows)).T
    query = (total[:head_rows] + bias[:head_rows, 0:1]) * HEAD_DIM**-0.5
    qkv_ref[0, 0] = query.astype(BF)
    key = total[head_rows : 2 * head_rows].astype(BF)
    qkv_ref[0, 1] = key
    value = (total[2 * head_rows :] + bias[head_rows:, 0:1]).astype(BF)
    qkv_ref[0, 2] = value
    key_t = key.T
    for start in range(0, SEQ, BLOCK):
        here = slice(start, start + BLOCK)
        scores = matmul(key_t, qkv_ref[0, 0, :, here])
        top = jnp.max(scores, axis=0, keepdims=True)
        weights = jnp.exp(scores - top)
        denom = jnp.sum(weights, axis=0, keepdims=True)
        out_ref[0, :, here] = matmul(value, weights.astype(BF)) * (1.0 / denom)
        norm_ref[0, :, here] = top + jnp.log(denom)


def turn_kernel(places, *refs):
    for ref, out_ref in zip(refs[:4], refs[4:]):
        out_ref[...] = ref[...].T


def out_far_kernel(places, early, late, own, far, own_ref, send_ref, full_ref, low_ref):
    heads, head_rows, _ = low_ref.shape
    half = far.shape[2]
    low_ref[: early.shape[0]] = early[...].astype(BF)
    low_ref[early.shape[0] :] = late[...].astype(BF)
    for head in range(heads):
        rows = slice(head * head_rows, (head + 1) * head_rows)
        full_ref[rows, part(places[2], half)] = own[head, 8:, :]
        full_ref[rows, part(1 - places[2], half)] = far[head, 8:, :]
    out_block(places, 3, low_ref, full_ref, send_ref)
    out_block(places, 2, low_ref, full_ref, own_ref)


def out_near_kernel(places, attended, full_ref, own_ref, send_ref):
    out_block(places, 1, attended, full_ref, send_ref)
    out_block(places, 0, attended, full_ref, own_ref)


def out_block(places, step, attended, full_ref, out_ref):
    rows = attended[:, :, part(places[0] ^ step, BLOCK)].reshape(-1, BLOCK)
    out_ref[...] = inner_rows(rows, full_ref[...]).astype(out_ref.dtype)


def norm1_kernel(places, near, core, got, x00, x01, x10, x11, vec, a_ref, low_ref, normed_ref, scale_ref):
    for side, pair in ((0, (x00, x01)), (1, (x10, x11))):
        for end, x in enumerate(pair):
            block = 2 * (places[3] ^ side) + (places[4] ^ end)
            a_ref[:, part(block, BLOCK)] = x[...].T.astype(F32)
    residual = a_ref[...] + (near[...] + core[...].astype(F32) + got[...].astype(F32) + vec[0:1])
    mean_rows = jnp.mean(residual, axis=1, keepdims=True)
    spread = jnp.mean(residual * residual, axis=1, keepdims=True) - mean_rows * mean_rows
    scale_rows = lax.rsqrt(spread + norm_eps)
    normed = (residual - mean_rows) * scale_rows
    values = normed * vec[1:2] + vec[2:3]
    a_ref[...] = values
    low_ref[...] = values.astype(BF)
    normed_ref[...] = normed
    scale_ref[...] = scale_rows


def back_of_norm(grad_in, normed, scale_rows, gain_vec):
    scaled = grad_in * gain_vec
    first = jnp.mean(scaled, axis=1, keepdims=True)
    second = jnp.mean(scaled * normed, axis=1, keepdims=True)
    return scale_rows * (scaled - first - normed * second)


def add_sums(sums_ref, *arrays):
    @pl.when(pl.program_id(0) == 0)
    def _():
        sums_ref[...] = jnp.zeros_like(sums_ref)

    for index, values in enumerate(arrays):
        sums_ref[index : index + 1] += jnp.sum(values, axis=0, keepdims=True)


def norm2_kernel(places, near, core, got, a_ref, c0, c1, c2, c3, vec, here_ref, send_ref, grad_ref, low_ref, sums_ref):
    for index, piece in enumerate((c0, c1, c2, c3)):
        block = 2 * (places[3] ^ (index >> 1)) + (places[4] ^ (index & 1))
        grad_ref[:, part(block, BLOCK)] = piece[...].T.astype(F32)
    branch = near[...] + core[...].astype(F32) + got[...].astype(F32) + vec[3:4]
    residual = a_ref[...] + branch
    mean_rows = jnp.mean(residual, axis=1, keepdims=True)
    spread = jnp.mean(residual * residual, axis=1, keepdims=True) - mean_rows * mean_rows
    scale_rows = lax.rsqrt(spread + norm_eps)
    normed = (residual - mean_rows) * scale_rows
    grad_out = grad_ref[...]
    grad = back_of_norm(grad_out, normed, scale_rows, vec[4:5])
    add_sums(sums_ref, grad, grad_out * normed, grad_out)
    grad_ref[...] = normed * vec[4:5] + vec[5:6]
    for side in range(2):
        for end, ref in ((0, here_ref), (1, send_ref)):
            block = 2 * (places[3] ^ side) + (places[4] ^ end)
            ref[side] = grad_ref[:, part(block, BLOCK)].T.astype(BF)
    grad_ref[...] = grad
    low_ref[...] = grad.astype(BF)


def norm1_back_kernel(places, near, core, got, grad2, normed_ref, scale_ref, vec, sums2, low_ref, sums_ref):
    grad_in = grad2[...] + (near[...] + core[...].astype(F32) + got[...].astype(F32))
    normed = normed_ref[...]
    grad = back_of_norm(grad_in, normed, scale_ref[...], vec[1:2])
    add_sums(sums_ref, grad, grad_in * normed, grad_in)
    sums_ref[3:6] = sums2[0:3]
    low_ref[...] = grad.astype(BF)


def weight_grad_kernel(places, left_near, left_far, r0, r1, r2, r3, mine_ref, sent_ref, right):
    half = mine_ref.shape[2]

    @pl.when(pl.program_id(0) == 0)
    def _():
        for index, rows in enumerate((r0, r1, r2, r3)):
            here = slice(index * BLOCK, (index + 1) * BLOCK)
            right[0, here] = rows[:, part(places[2], half)]
            right[1, here] = rows[:, part(1 - places[2], half)]

    left = jnp.concatenate([left_near[...], left_far[...]], 0)
    sent_ref[0, :BLOCK] = inner_rows(left, right[1]).astype(BF)
    mine_ref[0, :BLOCK] = inner_rows(left, right[0]).astype(BF)
    if mine_ref.shape[1] > BLOCK:
        sums = jnp.sum(left.astype(F32), axis=0, keepdims=True)
        sums = jnp.broadcast_to(jnp.concatenate([sums, sums], 1), (8, half)).astype(BF)
        sent_ref[0, BLOCK:] = sums
        mine_ref[0, BLOCK:] = sums


def out_back_kernel(places, d0, d1, d2, d3, full_ref, attended, grad_ref, mine_ref, sent_ref):
    heads, head_rows, _ = attended.shape
    blocks = (d0, d1, d2, d3)
    left = []
    for step, rows in enumerate(blocks):
        here = part(places[0] ^ step, BLOCK)
        grad = against(full_ref[...], rows[...]).astype(BF)
        grad_ref[:, :, here] = grad.reshape(heads, head_rows, BLOCK)
        left.append(attended[:, :, here].reshape(-1, BLOCK))
    width = mine_ref.shape[3]
    for ref, side in ((sent_ref, 1 - places[2]), (mine_ref, places[2])):
        for end in range(2):
            columns = part(2 * side + (places[4] ^ end), width)
            total = None
            for piece, rows in zip(left, blocks):
                product = matmul(piece, rows[:, columns])
                total = product if total is None else total + product
            ref[:, end] = total.astype(BF).reshape(heads, head_rows, width)


def attend_back_kernel(
    places, qkv_ref, grad_ref, norm_ref, attended, out_mine, out_sent, x00, x01, x10, x11, sums, out_ref, mine_ref, sent_ref, probs_low, scores_low
):
    head_rows = qkv_ref.shape[2]
    key = qkv_ref[0, 1]
    key_t = key.T
    value_t = qkv_ref[0, 2].T
    for start in range(0, SEQ, BLOCK):
        here = slice(start, start + BLOCK)
        grad = grad_ref[0, :, here]
        probs = jnp.exp(matmul(key_t, qkv_ref[0, 0, :, here]) - norm_ref[0, :, here])
        delta = jnp.sum(grad.astype(F32) * attended[0, :, here], axis=0, keepdims=True)
        grad_scores = (probs * (matmul(value_t, grad) - delta)).astype(BF)
        probs_low[:, here] = probs.astype(BF)
        scores_low[:, here] = grad_scores
        grad_query = matmul(key, grad_scores).astype(BF)
        out_ref[0, :head_rows, here] = (grad_query.astype(F32) * HEAD_DIM**-0.5).astype(BF)
    grad_key = matmul(scores_low[...], qkv_ref[0, 0].T)
    out_ref[0, head_rows : 2 * head_rows] = grad_key.T.astype(BF)
    grad_value = matmul(probs_low[...], grad_ref[0].T)
    out_ref[0, 2 * head_rows :] = grad_value.T.astype(BF)
    left = out_ref[0]
    bias = jnp.sum(left.astype(F32), axis=1, keepdims=True)
    bias = jnp.concatenate([bias[:head_rows], bias[2 * head_rows :]], 0)
    bias = jnp.broadcast_to(bias, (2 * head_rows, 2 * head_rows)).T[:8]
    bias = jnp.concatenate([bias, jnp.zeros((8, BLOCK - 2 * head_rows), F32)], 1)
    rows = 3 * head_rows
    for side, pair in ((0, (x00, x01)), (1, (x10, x11))):
        mine = (places[3] ^ side) == places[2]
        for end, x in enumerate(pair):
            weight = matmul(left, x[...]).astype(BF)
            block = sums[:, part(2 * (places[3] ^ side) + (places[4] ^ end), BLOCK)]
            extra = jnp.concatenate([block, bias], 0).astype(BF)

            @pl.when(mine)
            def _():
                mine_ref[0, end, :rows] = weight
                mine_ref[0, end, rows : rows + 16] = extra
                mine_ref[0, end, rows + 16 :] = out_mine[0, end]

            @pl.when(jnp.logical_not(mine))
            def _():
                sent_ref[0, end, :rows] = weight
                sent_ref[0, end, rows : rows + 16] = extra
                sent_ref[0, end, rows + 16 :] = out_sent[0, end]


def tail_sum_kernel(places, early_mine, early_got, late_mine, late_got, own_ref, *sums):
    own_ref[...] = early_mine[0].astype(F32) + early_got[0].astype(F32)
    blocks = [(early_mine, early_got, i) for i in range(1, early_mine.shape[0])]
    blocks += [(late_mine, late_got, i) for i in range(late_mine.shape[0])]
    for ref, (mine, got, head) in zip(sums, blocks):
        ref[...] = (mine[head].astype(F32) + got[head].astype(F32)).astype(BF)


def sum_kernel(places, mine, got, own_ref, *sums):
    own_ref[...] = mine[0].astype(F32) + got[0].astype(F32)
    for block, ref in enumerate(sums):
        ref[...] = (mine[block + 1].astype(F32) + got[block + 1].astype(F32)).astype(BF)


def last_ff_kernel(places, *refs):
    here, there = refs[-2:]
    inputs = refs[:-2]
    half = len(inputs) // 2
    first = 0
    for pieces in (inputs[:half], inputs[half:]):
        total = pieces[0][...]
        for ref in pieces[1:]:
            total = total + ref[...].astype(F32)
        rows, width = total.shape[0], total.shape[1] // 2
        left, right = total[:, :width], total[:, width:]
        is_left = places[4] == 0
        here[first : first + rows] = jnp.where(is_left, left, right).astype(BF)
        there[first : first + rows] = jnp.where(is_left, right, left).astype(BF)
        first += rows


def last_sum_kernel(places, own_ref, *refs):
    total = own_ref[...]
    for ref in refs[:-2]:
        total = total + ref[...].astype(F32)
    refs[-2][...] = total[0].astype(BF)
    refs[-1][...] = total[1].astype(BF)


def input_near_kernel(places, own0, own1, send0, send1, grads0, grads1, d0, d1, d2, d3, own_ref, send_ref):
    def product(first, second):
        pairs = ((first, grads0), (second, grads1))
        flat = [[ref[...].reshape(-1, ref.shape[2]) for ref in pair] for pair in pairs]
        return inner_rows(*flat[0]) + inner_rows(*flat[1])

    send_ref[...] = product(send0, send1).astype(BF)
    own_ref[...] = product(own0, own1)
    block = 2 * places[3] + places[4]
    for step, d in enumerate((d0, d1, d2, d3)):
        here = part(places[0] ^ step, BLOCK)
        own_ref[:, here] += d[:, part(block, BLOCK)].T.astype(F32)


def last_ff_out_kernel(places, p0, p1, p2, p3, down_out, up_out, bias_out):
    for step, ref in enumerate((p0, p1, p2, p3)):
        quarter = places[0] ^ step
        down_out[part(quarter, BLOCK), :] = ref[:BLOCK].astype(F32)
        up_out[:, part(quarter, BLOCK)] = ref[BLOCK : 2 * BLOCK].astype(F32).T
        bias_out[:, part(quarter, BLOCK)] = ref[2 * BLOCK :].astype(F32)[0:1]


def last_kernel(places, p0, p1, p2, p3, qkv_out, qv_out, norm_out, out_out, turned):
    parts = (p0, p1, p2, p3)
    head = turned.shape[0] // 4
    for piece in range(3):
        for step, ref in enumerate(parts):
            turned[part(places[0] ^ step, head), :] = ref[piece * head : (piece + 1) * head].astype(F32)
        qkv_out[piece] = turned[...].T
    extra = [ref[3 * head : 3 * head + 16].astype(F32) for ref in parts]
    norm_out[...] = extra[0][:8] + extra[1][:8] + extra[2][:8] + extra[3][:8]
    lines = [[], []]
    for quarter in range(4):
        line = sum(
            jnp.where((places[0] ^ step) == quarter, extra[step][8:9], 0.0) for step in range(4)
        )
        lines[0].append(line[:, :head])
        lines[1].append(line[:, head : 2 * head])
    qv_out[...] = jnp.concatenate([jnp.concatenate(line, 1) for line in lines], 0)
    for step, ref in enumerate(parts):
        out_out[part(places[0] ^ step, head), :] = ref[3 * head + 16 :].astype(F32)


def to_far_chip(own, send):
    return (own + flip(send, "dp").astype(F32)).astype(BF)


def gather_rows(payload):
    size = lax.axis_size("row")
    return [payload] + [shift(payload, "row", step) for step in range(1, size)]


def move_rows(sums):
    return [shift(block, "row", -1 - i) for i, block in enumerate(sums)]


def spread_weights(mine, other):
    return spread_cores(mine, flip(other, "t"))


def spread_cores(mine, got):
    near = jnp.stack([mine, got])
    far = flip(near, "dp")
    return near[0], far[0], near[1], far[1]


def fast_shards(
    tokens,
    w_qkv,
    b_qv,
    w_out,
    b_out,
    norm1_gain,
    norm1_shift,
    w_up,
    b_up,
    w_down,
    b_down,
    norm2_gain,
    norm2_shift,
    cotangent,
):
    core, chip = lax.axis_index("dp"), lax.axis_index("t")
    u_index, row = lax.axis_index("u"), lax.axis_index("row")
    rows = lax.axis_size("row")
    quarter = 2 * chip + core
    other_quarter = 2 * (1 - chip) + core
    places = jnp.stack([quarter, other_quarter, u_index, core, chip, row]).astype(jnp.int32)
    feats = tokens.shape[0]
    width = 4 * feats
    half = 2 * feats
    own_rows = SEQ // 4
    swap_cores = [(2 * d + u, 2 * u + d) for d in range(2) for u in range(2)]
    head_rows = w_out.shape[0] // 4
    qkv_rows, out_rows, ff_rows = 3 * head_rows, head_rows, w_down.shape[0] // 4

    x00 = lax.ppermute(tokens, ("dp", "u"), swap_cores)

    attn_rows = qkv_rows + 16 + out_rows
    attn_keep, attn_send = kernel_call(
        prepare_attn_kernel,
        "prepare_attn",
        [((attn_rows, feats), BF)] * 2,
        places,
        w_qkv.transpose(1, 0, 2),
        b_qv,
        w_out,
        b_out,
        norm1_gain,
        norm1_shift,
        b_down,
        norm2_gain,
        norm2_shift,
        scratch=[pltpu.VMEM((3, 4 * head_rows, feats), BF)],
        vmem=60,
    )
    attn_got = flip(attn_send, "t")
    ff_keep, ff_send = kernel_call(
        prepare_ff_kernel, "prepare_ff", [((2 * ff_rows, feats), BF)] * 2, places, after(w_up, attn_send), w_down, vmem=60
    )
    ff_got = flip(ff_send, "t")
    attn_got = after(attn_got, x00)
    cot = lax.ppermute(after(cotangent, x00), ("dp", "u"), swap_cores)
    x01 = flip(x00, "t")
    x10, x11 = flip(x00, "dp"), flip(x01, "dp")
    cot = after(cot, x01)
    cot_parts = [cut(cot, quarter ^ j, own_rows, 1) for j in range(4)]
    cot_far = flip(jnp.stack([cot_parts[2], cot_parts[3]]), "t")
    cot_near = flip(jnp.stack([cot_parts[1], cot_far[1]]), "dp")

    qkv_part = jnp.stack([attn_keep[: qkv_rows + 8], attn_got[: qkv_rows + 8]])
    ff_got = after(ff_got, qkv_part)
    qkv_own = jnp.stack(gather_rows(qkv_part))
    attn_both = in_order(chip, attn_keep[qkv_rows + 8 :], attn_got[qkv_rows + 8 :], 1)
    ff_both = in_order(chip, ff_keep, ff_got, 1)
    up_bias = lax.dynamic_index_in_dim(b_up.reshape(4, -1), quarter, 0, True)
    up_bias = jnp.pad(up_bias, ((0, 7), (0, half - ff_rows)))
    mixed_part = jnp.concatenate([attn_both, ff_both[:ff_rows], up_bias])
    mixed_pieces = gather_rows(after(mixed_part, qkv_own))
    qkv_far = flip(after(qkv_own, x01), "u")

    x_blocks = (x00, x01, x10, x11)
    pair_of_heads = rows // 2

    def attend(first, far_half):
        def of(shape):
            return pl.BlockSpec(
                shape, lambda step, places: (first + step,) + (0,) * (len(shape) - 1)
            )

        return kernel_call(
            attend_kernel,
            "attend",
            [
                ((pair_of_heads, 3, head_rows, SEQ), BF),
                ((pair_of_heads, head_rows, SEQ), F32),
                ((pair_of_heads, 1, SEQ), F32),
            ]
            + [((pair_of_heads, qkv_rows, feats), BF)] * 4,
            places,
            *x_blocks,
            qkv_own,
            far_half,
            grid=pair_of_heads,
            specs=[fixed((feats, SEQ))] * 4 + [of((1, 2, qkv_rows + 8, feats))] * 2,
            out_specs=[
                stepped((1, 3, head_rows, SEQ), 0),
                stepped((1, head_rows, SEQ), 0),
                stepped((1, 1, SEQ), 0),
            ]
            + [stepped((1, qkv_rows, feats), 0)] * 4,
            vmem=28,
            long=True,
        )

    qkv_early, attended_early, norm_early, *weight_early = attend(0, qkv_far)
    mixed_own = jnp.stack(after(mixed_pieces, norm_early, cot_near))
    down_pieces = gather_rows(after(ff_both[ff_rows:], mixed_own))
    vec_rows = 8 + out_rows
    out_own, up_own = mixed_own[:, :vec_rows], mixed_own[:, vec_rows:]
    out_far = flip(out_own, "u")
    up_far = flip(up_own, "u")
    far_late = after(qkv_far, mixed_own)
    qkv_late, attended_late, norm_late, *weight_late = attend(pair_of_heads, far_late)
    attended_late = after(attended_late, down_pieces[1], down_pieces[3:])
    bias_up = up_own[:, ff_rows, :ff_rows].reshape(1, -1).astype(F32)
    vec = in_order(u_index, out_own[0, :8], out_far[0, :8], 1).astype(F32)
    up_pair = [x[:, :ff_rows].reshape(rows * ff_rows, half) for x in (up_own, up_far)]
    up_full = in_order(u_index, *up_pair, 1)

    row_block = (own_rows, width)
    pair_outs = [(row_block, F32), (row_block, BF)]
    far_own, far_send, out_full, low_attended = kernel_call(
        out_far_kernel,
        "out_far",
        pair_outs + [((rows * head_rows, width), BF), ((rows, head_rows, SEQ), BF)],
        places,
        attended_early,
        attended_late,
        out_own,
        out_far,
    )
    sent = to_far_chip(far_own, far_send)
    near_attended = after(low_attended, sent, up_far, down_pieces)
    got = flip(sent, "t")
    near_own, near_send = kernel_call(
        out_near_kernel, "out_near", pair_outs, places, near_attended, out_full
    )
    down_own = jnp.stack(after(down_pieces, near_own))
    down_far = flip(down_own, "u").reshape(rows * ff_rows, half)
    down_full = in_order(u_index, down_own.reshape(rows * ff_rows, half), down_far, 1)
    near_got = flip(near_send, "dp")
    got = after(got, near_got, up_far, down_own)
    chunk = own_rows // 2
    row_chunk = stepped((chunk, width), 0)
    own_tokens = pl.BlockSpec((feats, chunk), lambda step, places: (0, 2 * places[0] + step))
    normed_a, low_a, normed1, scale1 = kernel_call(
        norm1_kernel,
        "norm1",
        [(row_block, F32), (row_block, BF), (row_block, F32), ((own_rows, 1), F32)],
        places,
        near_own,
        near_got,
        got,
        *x_blocks,
        vec,
        grid=2,
        specs=[row_chunk] * 3 + [own_tokens] * 4 + [fixed((8, width))],
        out_specs=[row_chunk] * 3 + [stepped((chunk, 1), 0)],
    )

    def up(rows_in):
        pre = against(rows_in, up_full) + bias_up
        cdf = 0.5 * (1.0 + lax.erf(pre * (0.5**0.5)))
        slope = cdf + pre * (jnp.exp(-0.5 * pre * pre) * 0.3989422804014327)
        return (pre * cdf).astype(BF), slope

    a0, a1, a2 = low_a, flip(low_a, "dp"), flip(low_a, "t")
    hidden_near, slope_near = up(jnp.concatenate([a0, a1]))
    a2 = after(a2, hidden_near)
    a3 = flip(a2, "dp")
    hidden_far, slope_far = up(jnp.concatenate([a2, a3]))
    far_send = matmul(hidden_far[own_rows:], down_full).astype(BF)
    sent = to_far_chip(matmul(hidden_far[:own_rows], down_full), far_send)
    near_hidden = after(hidden_near, sent)
    token_rows = kernel_call(
        turn_kernel, "turn", [((SEQ, feats), BF)] * 4, places, *after(x_blocks, near_hidden)
    )
    got = flip(sent, "t")
    near_got = flip(matmul(near_hidden[own_rows:], down_full).astype(BF), "dp")
    near_own = matmul(near_hidden[:own_rows], down_full)
    got = after(got, near_got, token_rows)
    turned_chunk = stepped((feats, chunk), 1)
    pair_chunk = stepped((2, feats, chunk), 2)
    result_here, result_send, grad_r2, low_g, sums2 = kernel_call(
        norm2_kernel,
        "norm2",
        [((2, feats, own_rows), BF)] * 2 + [(row_block, F32), (row_block, BF), ((8, width), F32)],
        places,
        near_own,
        near_got,
        got,
        normed_a,
        cot_parts[0],
        cot_far[0],
        cot_near[0],
        cot_near[1],
        vec,
        grid=2,
        specs=[row_chunk] * 4 + [turned_chunk] * 4 + [fixed((8, width))],
        out_specs=[pair_chunk] * 2 + [row_chunk] * 2 + [fixed((8, width))],
    )

    two_blocks = 2 * own_rows

    def weight_grad(near, far, blocks, extra):
        shape = (rows, ff_rows + extra, half)
        return kernel_call(
            weight_grad_kernel,
            "weight_grad",
            [(shape, BF)] * 2,
            places,
            near,
            far,
            *blocks,
            grid=rows,
            specs=[stepped((two_blocks, ff_rows), 1)] * 2 + [fixed(row_block)] * 4,
            out_specs=[stepped((1, *shape[1:]), 0)] * 2,
            scratch=[pltpu.VMEM((2, SEQ, half), BF)],
            long=True,
        )

    g0, g1, g2 = low_g, flip(low_g, "dp"), flip(low_g, "t")
    grad_pre_near = (against(jnp.concatenate([g0, g1]), down_full) * slope_near).astype(BF)
    g2 = after(g2, grad_pre_near)
    g3 = flip(g2, "dp")
    grad_pre_far = (against(jnp.concatenate([g2, g3]), down_full) * slope_far).astype(BF)
    far_send = matmul(grad_pre_far[own_rows:], up_full).astype(BF)
    sent = to_far_chip(matmul(grad_pre_far[:own_rows], up_full), far_send)
    near_pre = after(grad_pre_near, sent)
    got = flip(sent, "t")
    near_got = flip(matmul(near_pre[own_rows:], up_full).astype(BF), "dp")
    near_own = matmul(near_pre[:own_rows], up_full)
    hiddens, pres = after(((hidden_near, hidden_far), (near_pre, grad_pre_far)), near_own)
    down_mine, down_sent = weight_grad(*hiddens, (g0, g1, g2, g3), 0)
    down_got = flip(down_sent, "u")
    up_mine, up_sent = weight_grad(*pres, (a0, a1, a2, a3), 8)
    got = after(got, near_got, up_sent)
    low_r1, sums = kernel_call(
        norm1_back_kernel,
        "norm1_back",
        [(row_block, BF), ((8, width), F32)],
        places,
        near_own,
        near_got,
        got,
        grad_r2,
        normed1,
        scale1,
        vec,
        sums2,
        grid=2,
        specs=[row_chunk] * 5 + [stepped((chunk, 1), 0)] + [fixed((8, width))] * 2,
        out_specs=[row_chunk, fixed((8, width))],
    )

    d0, d1, d2 = low_r1, flip(low_r1, "dp"), flip(low_r1, "t")
    down_got = after(down_got, low_r1)
    up_sent, down_got = lax.optimization_barrier((up_sent, down_got))
    up_got = flip(up_sent, "u")
    d2 = after(d2, down_got)

    def sums_of(mine, got):
        shape = mine.shape[1:]
        return kernel_call(
            sum_kernel, "sum", [(shape, F32)] + [(shape, BF)] * (rows - 1), places, mine, got
        )

    d3 = flip(d2, "dp")
    d_blocks = (d0, d1, d2, d3)
    out_shape = (rows, 2, out_rows, feats)
    grad_att, out_mine, out_sent = kernel_call(
        out_back_kernel,
        "out_back",
        [((rows, head_rows, SEQ), BF)] + [(out_shape, BF)] * 2,
        places,
        *d_blocks,
        out_full,
        low_attended,
    )
    down_total, *down_sums = sums_of(down_mine, after(down_got, grad_att))
    grad_att = after(grad_att, down_sums)
    down_moved = move_rows(down_sums)
    extra_rows = qkv_rows + 16 + out_rows

    def attend_back(first, grad, qkv, log_norm, attended):
        def of(shape):
            return pl.BlockSpec(
                shape, lambda step, places: (first + step,) + (0,) * (len(shape) - 1)
            )

        return kernel_call(
            attend_back_kernel,
            "attend_back",
            [((pair_of_heads, qkv_rows, SEQ), BF)]
            + [((pair_of_heads, 2, extra_rows, feats), BF)] * 2,
            places,
            qkv,
            grad,
            log_norm,
            attended,
            out_mine,
            out_sent,
            *token_rows,
            sums,
            grid=pair_of_heads,
            specs=[
                stepped((1, 3, head_rows, SEQ), 0),
                of((1, head_rows, SEQ)),
                stepped((1, 1, SEQ), 0),
                stepped((1, head_rows, SEQ), 0),
                of((1, 2, out_rows, feats)),
                of((1, 2, out_rows, feats)),
            ]
            + [fixed((SEQ, feats))] * 4
            + [fixed((8, width))],
            out_specs=[stepped((1, qkv_rows, SEQ), 0)]
            + [stepped((1, 2, extra_rows, feats), 0)] * 2,
            scratch=[pltpu.VMEM((SEQ, SEQ), BF)] * 2,
            vmem=30,
            long=True,
        )

    result_far = flip(after(result_send, d3), "t")
    result_near = flip(jnp.stack([result_here[1], result_far[1]]), "dp")
    result_parts = [result_here[0], result_near[0], result_far[0], result_near[1]]

    grads_late, late_mine, late_sent = attend_back(
        pair_of_heads, grad_att, qkv_late, norm_late, attended_late
    )
    late_got = flip(late_sent, "u")
    up_total, *up_sums = sums_of(up_mine, after(up_got, late_sent))
    up_moved = move_rows(up_sums)
    early_att = after(grad_att, up_sums, down_moved, result_near)
    grads_early, early_mine, early_sent = attend_back(
        0, early_att, qkv_early, norm_early, attended_early
    )
    early_got = flip(after(early_sent, up_moved[0], up_moved[2:]), "u")
    sum_shape = (2, extra_rows, feats)
    early_own, *tail_sums = kernel_call(
        tail_sum_kernel,
        "tail_sum",
        [(sum_shape, F32)] + [(sum_shape, BF)] * (rows - 1),
        places,
        early_mine,
        early_got,
        late_mine,
        after(late_got, early_sent, up_moved),
    )
    moved = move_rows(tail_sums)

    def back_to(index, grads_early):
        pairs = ((weight_early[index], grads_early), (weight_late[index], grads_late))
        products = [
            inner_rows(w.reshape(-1, feats), grads.reshape(-1, SEQ)) for w, grads in pairs
        ]
        return products[0] + products[1]

    grads_now = after(grads_early, tail_sums)
    far_send = back_to(3, grads_now).astype(BF)
    sent = to_far_chip(back_to(1, grads_now), far_send)
    got = flip(sent, "t")
    near_own, near_send = kernel_call(
        input_near_kernel,
        "input_near",
        [((feats, SEQ), F32), ((feats, SEQ), BF)],
        places,
        weight_early[0],
        weight_late[0],
        weight_early[2],
        weight_late[2],
        after(grads_early, sent),
        grads_late,
        *d_blocks,
        vmem=24,
    )
    near_got = flip(near_send, "dp")
    result_seq = after(four_in_order(core, chip, result_parts, 1), tail_sums)
    result_out = lax.ppermute(result_seq, ("dp", "u"), swap_cores)
    ff_sums = kernel_call(
        last_ff_kernel,
        "last_ff",
        [((2 * ff_rows + 8, feats), BF)] * 2,
        places,
        after(down_total, near_own, result_out),
        *down_moved,
        up_total,
        *up_moved,
    )
    ff_got = flip(ff_sums[1], "t")
    got = after(got, moved, ff_got)
    grad_in = (near_own + near_got.astype(F32) + got.astype(F32)).astype(BF)
    grad_tokens = lax.ppermute(grad_in, ("dp", "u"), swap_cores)
    last_sums = kernel_call(
        last_sum_kernel,
        "last_sum",
        [(sum_shape[1:], BF)] * 2,
        places,
        after(early_own, grad_in),
        *moved,
    )
    last_got = flip(last_sums[1], "t")
    down_out, up_out, up_bias_out = kernel_call(
        last_ff_out_kernel,
        "last_ff_out",
        [((4 * ff_rows, feats), F32), ((feats, 4 * ff_rows), F32), ((1, 4 * ff_rows), F32)],
        places,
        *spread_cores(after(ff_sums[0], last_got), ff_got),
    )
    last_parts = spread_cores(after(last_sums[0], grad_tokens), last_got)
    grad_tokens = after(grad_tokens, last_parts[2]).astype(F32)
    qkv_out, qv_out, norm_out, out_out = kernel_call(
        last_kernel,
        "last",
        [
            ((3, feats, 4 * head_rows), F32),
            ((2, 4 * head_rows), F32),
            ((8, feats), F32),
            ((4 * out_rows, feats), F32),
        ],
        places,
        *last_parts,
        scratch=[pltpu.VMEM((4 * head_rows, feats), F32)],
    )
    return (
        result_out,
        grad_tokens,
        qkv_out.transpose(1, 0, 2),
        qv_out,
        out_out,
        norm_out[0],
        norm_out[1],
        norm_out[2],
        up_out,
        up_bias_out[0],
        down_out,
        norm_out[3],
        norm_out[4],
        norm_out[5],
    )


def solution(mesh):
    sizes = dict(mesh.shape)
    grouped = sizes["dp"] == 2 and sizes["col"] == 4 and D % (4 * sizes["row"] * HEAD_DIM) == 0
    if grouped:
        devices = mesh.devices.reshape(sizes["dp"], sizes["row"], 2, 2)
        inner_mesh, col, body = Mesh(devices, ("dp", "row", "u", "t")), ("u", "t"), fast_shards
    else:
        inner_mesh, col, body = mesh, "col", shards
    tokens_spec = P(col, ("dp", "row"))
    return jax.shard_map(
        body,
        mesh=inner_mesh,
        in_specs=(
            tokens_spec,
            P(col, None, "row"),
            P(None, "row"),
            P("row", col),
            P(col),
            P(col),
            P(col),
            P(col, "row"),
            P("row"),
            P("row", col),
            P(col),
            P(col),
            P(col),
            tokens_spec,
        ),
        out_specs=(
            tokens_spec,
            tokens_spec,
            P(col, None, "row"),
            P(None, "row"),
            P("row", col),
            P(col),
            P(col),
            P(col),
            P(col, "row"),
            P("row"),
            P("row", col),
            P(col),
            P(col),
            P(col),
        ),
        check_vma=False,
    )
```

profile of v0, /device:TPU:1, one launch (start us, length us, event | category | flops | bytes accessed | tf_op | source)
XLA Modules:
  0.0 328.4 jit_solution(13900088079340978511)
XLA Ops:
  0.6 4.5 %collective-permute-start = (bf16[256,1024]{1,0:T(8,128)(2,1)}, bf16[256,1024]{1,0:T(8,128)(2,1)S(1)}, u32[]{:S(2)}, u32[]{:S(2)}) collective-permute-start(bf16[256,1024]{1,0:T(8,128)(2,1)} %param.14), channel_id=1, source_target_pairs={{0,0},{2,16},{16,2},{18,18},{1,1},{3,17},{17,3},{19,19},{4,4},{6,2... | collective-permute-start | bytes 1572872 | tf_op jit(solution)/shard_map/ppermute | solution.py:699
  5.8 2.7 prepare_attn.1
  9.7 2.7 prepare_ff.1
  14.3 2.5 collective-permute-start.13
  18.1 3.4 %collective-permute-start.7 = (bf16[2,200,256]{2,1,0:T(8,128)(2,1)S(1)}, bf16[2,200,256]{2,1,0:T(8,128)(2,1)S(1)}, u32[]{:S(2)}, u32[]{:S(2)}) collective-permute-start(bf16[2,200,256]{2,1,0:T(8,128)(2,1)S(1)} %get-tuple-element.305), channel_id=1, source_target_pairs={{0,12},{4,0},{8,4},{12,8},{1,13},{5,1},{9,5},{13,9},{2,14},{6,2},{... | collective-permute-start | bytes 614408 | tf_op jit(solution)/shard_map/ppermute | solution.py:273
  23.2 3.3 collective-permute-done.7
  26.5 11.8 %collective-permute-done.6 = bf16[2,200,256]{2,1,0:T(8,128)(2,1)S(1)} collective-permute-done((bf16[2,200,256]{2,1,0:T(8,128)(2,1)S(1)}, bf16[2,200,256]{2,1,0:T(8,128)(2,1)S(1)}, u32[]{:S(2)}, u32[]{:S(2)}) %collective-permute-start.6) | collective-permute-done | bytes 204832 | tf_op jit(solution)/shard_map/ppermute | solution.py:273
  41.4 5.3 %collective-permute-done.14 = bf16[2,256,256]{2,1,0:T(8,128)(2,1)S(1)} collective-permute-done((bf16[2,256,256]{2,1,0:T(8,128)(2,1)S(1)}, bf16[2,256,256]{2,1,0:T(8,128)(2,1)S(1)}, u32[]{:S(2)}, u32[]{:S(2)}) %collective-permute-start.14) | collective-permute-done | bytes 262176 | tf_op jit(solution)/shard_map/ppermute | solution.py:268
  46.7 2.4 collective-permute-start.11
  50.6 8.0 %collective-permute-done.8.far = bf16[4,2,200,256]{3,2,1,0:T(8,128)(2,1)S(1)} collective-permute-done((bf16[4,2,200,256]{3,2,1,0:T(8,128)(2,1)S(1)}, bf16[4,2,200,256]{3,2,1,0:T(8,128)(2,1)S(1)}, u32[]{:S(2)}, u32[]{:S(2)}) %collective-permute-start.8) | collective-permute-done | bytes 819232 | tf_op jit(solution)/shard_map/ppermute | solution.py:268
  58.7 7.4 %attend.2 = (bf16[2,3,64,1024]{3,2,1,0:T(8,128)(2,1)S(1)}, f32[2,64,1024]{2,1,0:T(8,128)S(1)}, f32[2,1,1024]{2,1,0:T(1,128)S(1)}, bf16[2,192,256]{2,1,0:T(8,128)...) custom-call(s32[6]{0:T(128)S(1)} %copy-done.44, ...), custom_call_target="tpu_custom_call" | custom-call | flops 10000000000 | bytes 100000000 | tf_op jit(solution)/shard_map/attend/pallas_call | solution.py:301
  66.2 7.1 %collective-permute-done.11 = bf16[336,512]{1,0:T(8,128)(2,1)S(1)} collective-permute-done((bf16[336,512]{1,0:T(8,128)(2,1)S(1)}, bf16[336,512]{1,0:T(8,128)(2,1)S(1)}, u32[]{:S(2)}, u32[]{:S(2)}) %collective-permute-start.11) | collective-permute-done | bytes 344096 | tf_op jit(solution)/shard_map/ppermute | solution.py:273
  75.4 1.8 collective-permute-start.18
  77.2 7.4 %attend.3 = (bf16[2,3,64,1024]{3,2,1,0:T(8,128)(2,1)S(1)}, f32[2,64,1024]{2,1,0:T(8,128)S(1)}, f32[2,1,1024]{2,1,0:T(1,128)S(1)}, bf16[2,192,256]{2,1,0:T(8,128)...) custom-call(s32[6]{0:T(128)S(1)} %copy-done.44, ...), custom_call_target="tpu_custom_call" | custom-call | flops 10000000000 | bytes 100000000 | tf_op jit(solution)/shard_map/attend/pallas_call | solution.py:301
  84.8 2.6 collective-permute-done.16
  93.6 10.1 %collective-permute-done.21 = bf16[256,512]{1,0:T(8,128)(2,1)S(1)} collective-permute-done((bf16[256,512]{1,0:T(8,128)(2,1)S(1)}, bf16[256,512]{1,0:T(8,128)(2,1)S(1)}, u32[]{:S(2)}, u32[]{:S(2)}) %collective-permute-start.21) | collective-permute-done | bytes 262176 | tf_op jit(solution)/shard_map/ppermute | solution.py:273
  103.7 2.5 collective-permute-done.20
  108.0 2.1 collective-permute-start.22
  113.8 2.5 norm1.1
  119.7 10.2 %collective-permute-done.25.r2 = bf16[256,1024]{1,0:T(8,128)(2,1)S(1)} collective-permute-done((bf16[256,1024]{1,0:T(8,128)(2,1)S(1)}, bf16[256,1024]{1,0:T(8,128)(2,1)S(1)}, u32[]{:S(2)}, u32[]{:S(2)}) %collective-permute-start.25) | collective-permute-done | bytes 524320 | tf_op jit(solution)/shard_map/ppermute | solution.py:268
  130.9 6.1 %collective-permute-done.27 = bf16[4,256,512]{2,1,0:T(8,128)(2,1)S(1)} collective-permute-done((bf16[4,256,512]{2,1,0:T(8,128)(2,1)S(1)}, bf16[4,256,512]{2,1,0:T(8,128)(2,1)S(1)}, u32[]{:S(2)}, u32[]{:S(2)}) %collective-permute-start.27) | collective-permute-done | bytes 1048608 | tf_op jit(solution)/shard_map/ppermute | solution.py:268
  146.9 10.3 %collective-permute-done.30.got = bf16[256,1024]{1,0:T(8,128)(2,1)S(1)} collective-permute-done((bf16[256,1024]{1,0:T(8,128)(2,1)S(1)}, bf16[256,1024]{1,0:T(8,128)(2,1)S(1)}, u32[]{:S(2)}, u32[]{:S(2)}) %collective-permute-start.30) | collective-permute-done | bytes 524320 | tf_op jit(solution)/shard_map/ppermute | solution.py:268
  157.2 2.8 norm2.1
  162.5 1.8 fusion.5.left_near
  164.3 10.2 %collective-permute-done.32.r2 = bf16[256,1024]{1,0:T(8,128)(2,1)S(1)} collective-permute-done((bf16[256,1024]{1,0:T(8,128)(2,1)S(1)}, bf16[256,1024]{1,0:T(8,128)(2,1)S(1)}, u32[]{:S(2)}, u32[]{:S(2)}) %collective-permute-start.32) | collective-permute-done | bytes 524320 | tf_op jit(solution)/shard_map/ppermute | solution.py:268
  176.9 1.8 fusion.11.left_far
  185.4 4.0 %weight_grad.3 = (bf16[4,256,512]{2,1,0:T(8,128)(2,1)S(1)}, bf16[4,256,512]{2,1,0:T(8,128)(2,1)S(1)}) custom-call(s32[6]{0:T(128)S(1)} %copy-done.44, bf16[512,1024]{1,0:T(8,128)(2,1)S(1)} %get-tuple-element.205.left_near, bf16[512,1024]{1,0:T(8,128)(2,1)S(1)} %get-tuple-element.206.left_far, bf16[256,1024]{1,0:T(8,128)(2,1)S(1)} %get-tuple-element.193.r0, ...), custom_call_target="tpu_custom_call" | custom-call | flops 10000000000 | bytes 100000000 | tf_op jit(solution)/shard_map/weight_grad/pallas_call | solution.py:301
  190.9 4.0 %weight_grad.2 = (bf16[4,264,512]{2,1,0:T(8,128)(2,1)S(1)}, bf16[4,264,512]{2,1,0:T(8,128)(2,1)S(1)}) custom-call(s32[6]{0:T(128)S(1)} %copy-done.44, bf16[512,1024]{1,0:T(8,128)(2,1)S(1)} %fusion.5.left_near, bf16[512,1024]{1,0:T(8,128)(2,1)S(1)} %fusion.11.left_far, bf16[256,1024]{1,0:T(8,128)(2,1)S(1)} %get-tuple-element.178.r0, ...), custom_call_target="tpu_custom_call" | custom-call | flops 10000000000 | bytes 100000000 | tf_op jit(solution)/shard_map/weight_grad/pallas_call | solution.py:301
  195.0 1.7 collective-permute-done.36.got
  199.5 14.7 %collective-permute-done.38.got = bf16[4,256,512]{2,1,0:T(8,128)(2,1)S(1)} collective-permute-done((bf16[4,256,512]{2,1,0:T(8,128)(2,1)S(1)}, bf16[4,256,512]{2,1,0:T(8,128)(2,1)S(1)}, u32[]{:S(2)}, u32[]{:S(2)}) %collective-permute-start.38) | collective-permute-done | bytes 1048608 | tf_op jit(solution)/shard_map/ppermute | solution.py:268
  218.3 1.9 out_back.1
  221.8 1.9 collective-permute-start.44
  225.7 10.3 %attend_back.2 = (bf16[2,192,1024]{2,1,0:T(8,128)(2,1)S(1)}, bf16[2,2,272,256]{3,2,1,0:T(8,128)(2,1)S(1)}, bf16[2,2,272,256]{3,2,1,0:T(8,128)(2,1)}) custom-call(s32[6]{0:T(128)S(1)} %copy-done.44, bf16[2,3,64,1024]{3,2,1,0:T(8,128)(2,1)S(1)} %copy-done.48, bf16[4,64,1024]{2,1,0:T(8,128)(2,1)S(1)} %get-tuple-element.232.grad_ref, ...), custom_call_target="tpu_custom_call" | custom-call | flops 10000000000 | bytes 100000000 | tf_op jit(solution)/shard_map/attend_back/pallas_call | solution.py:301
  236.0 5.5 %collective-permute-done.43.got = bf16[4,264,512]{2,1,0:T(8,128)(2,1)S(1)} collective-permute-done((bf16[4,264,512]{2,1,0:T(8,128)(2,1)S(1)}, bf16[4,264,512]{2,1,0:T(8,128)(2,1)S(1)}, u32[]{:S(2)}, u32[]{:S(2)}) %collective-permute-start.43) | collective-permute-done | bytes 1081376 | tf_op jit(solution)/shard_map/ppermute | solution.py:268
  245.2 1.9 collective-permute-start.47
  248.6 10.0 %attend_back.3 = (bf16[2,192,1024]{2,1,0:T(8,128)(2,1)S(1)}, bf16[2,2,272,256]{3,2,1,0:T(8,128)(2,1)S(1)}, bf16[2,2,272,256]{3,2,1,0:T(8,128)(2,1)}) custom-call(s32[6]{0:T(128)S(1)} %copy-done.44, bf16[2,3,64,1024]{3,2,1,0:T(8,128)(2,1)S(1)} %copy-done.46, bf16[4,64,1024]{2,1,0:T(8,128)(2,1)S(1)} %get-tuple-element.232.grad_ref, ...), custom_call_target="tpu_custom_call" | custom-call | flops 10000000000 | bytes 100000000 | tf_op jit(solution)/shard_map/attend_back/pallas_call | solution.py:301
  262.6 12.0 %collective-permute-done.51.refs_6_ = bf16[264,512]{1,0:T(8,128)(2,1)} collective-permute-done((bf16[264,512]{1,0:T(8,128)(2,1)}, bf16[264,512]{1,0:T(8,128)(2,1)}, u32[]{:S(2)}, u32[]{:S(2)}) %collective-permute-start.51) | collective-permute-done | bytes 270368 | tf_op jit(solution)/shard_map/ppermute | solution.py:273
  274.6 2.1 tail_sum.1
  279.4 2.7 collective-permute-start.56
  282.2 2.8 collective-permute-start.52
  286.8 2.0 input_near.1
  288.9 4.0 %collective-permute-done.52 = bf16[256,1024]{1,0:T(8,128)(2,1)S(1)} collective-permute-done((bf16[256,1024]{1,0:T(8,128)(2,1)S(1)}, bf16[256,1024]{1,0:T(8,128)(2,1)S(1)}, u32[]{:S(2)}, u32[]{:S(2)}) %collective-permute-start.52) | collective-permute-done | bytes 524320 | tf_op jit(solution)/shard_map/ppermute | solution.py:1051
  293.0 1.8 last_ff.1
  296.1 13.5 %collective-permute-done.57.refs_1_ = bf16[2,272,256]{2,1,0:T(8,128)(2,1)S(1)} collective-permute-done((bf16[2,272,256]{2,1,0:T(8,128)(2,1)S(1)}, bf16[2,272,256]{2,1,0:T(8,128)(2,1)S(1)}, u32[]{:S(2)}, u32[]{:S(2)}) %collective-permute-start.57) | collective-permute-done | bytes 278560 | tf_op jit(solution)/shard_map/ppermute | solution.py:273
  310.9 3.0 collective-permute-start.60
  316.9 4.5 %collective-permute-done.60 = bf16[256,1024]{1,0:T(8,128)(2,1)S(1)} collective-permute-done((bf16[256,1024]{1,0:T(8,128)(2,1)S(1)}, bf16[256,1024]{1,0:T(8,128)(2,1)S(1)}, u32[]{:S(2)}, u32[]{:S(2)}) %collective-permute-start.60) | collective-permute-done | bytes 524320 | tf_op jit(solution)/shard_map/ppermute | solution.py:1065
  322.6 2.1 last_ff_out.1
  324.8 1.8 last.1
  (294 shorter events, 84.4 us)
Async XLA Ops:
  0.6 13.7 %collective-permute-start = (bf16[256,1024]{1,0:T(8,128)(2,1)}, bf16[256,1024]{1,0:T(8,128)(2,1)S(1)}, u32[]{:S(2)}, u32[]{:S(2)}) collective-permute-start(bf16[256,1024]{1,0:T(8,128)(2,1)} %param.14), channel_id=1, source_target_pairs={{0,0},{2,16},{16,2},{18,18},{1,1},{3,17},{17,3},{19,19},{4,4},{6,2... | collective-permute-start | bytes 1572872 | tf_op jit(solution)/shard_map/ppermute | solution.py:699
  12.5 9.1 %collective-permute-start.9 = (bf16[512,256]{1,0:T(8,128)(2,1)}, bf16[512,256]{1,0:T(8,128)(2,1)S(1)}, u32[]{:S(2)}, u32[]{:S(2)}) collective-permute-start(bf16[512,256]{1,0:T(8,128)(2,1)} %get-tuple-element.152), channel_id=1, source_target_pairs={{0,1},{1,0},{2,3},{3,2},{4,5},{5,4},{6,7},{7,6},{8,9},{9,8},{10,11... | collective-permute-start | bytes 786440 | tf_op jit(solution)/shard_map/ppermute | solution.py:268
  14.3 24.1 %collective-permute-start.13 = (bf16[256,1024]{1,0:T(8,128)(2,1)}, bf16[256,1024]{1,0:T(8,128)(2,1)S(1)}, u32[]{:S(2)}, u32[]{:S(2)}) collective-permute-start(bf16[256,1024]{1,0:T(8,128)(2,1)} %param.27), channel_id=1, source_target_pairs={{0,0},{2,16},{16,2},{18,18},{1,1},{3,17},{17,3},{19,19},{4,4},{6,2... | collective-permute-start | bytes 1572872 | tf_op jit(solution)/shard_map/ppermute | solution.py:725
  16.8 21.6 %collective-permute-start.1 = (bf16[256,1024]{1,0:T(8,128)(2,1)S(1)}, bf16[256,1024]{1,0:T(8,128)(2,1)S(1)}, u32[]{:S(2)}, u32[]{:S(2)}) collective-permute-start(bf16[256,1024]{1,0:T(8,128)(2,1)S(1)} %collective-permute-done.x00.refs_0_), channel_id=1, source_target_pairs={{0,1},{1,0},{2,3},{3,2},{4,5},{5,4},{6,7},{7,6},{8,9},{9,8},{10,11... | collective-permute-start | bytes 1572872 | tf_op jit(solution)/shard_map/ppermute | solution.py:268
  18.1 8.3 %collective-permute-start.7 = (bf16[2,200,256]{2,1,0:T(8,128)(2,1)S(1)}, bf16[2,200,256]{2,1,0:T(8,128)(2,1)S(1)}, u32[]{:S(2)}, u32[]{:S(2)}) collective-permute-start(bf16[2,200,256]{2,1,0:T(8,128)(2,1)S(1)} %get-tuple-element.305), channel_id=1, source_target_pairs={{0,12},{4,0},{8,4},{12,8},{1,13},{5,1},{9,5},{13,9},{2,14},{6,2},{... | collective-permute-start | bytes 614408 | tf_op jit(solution)/shard_map/ppermute | solution.py:273
  21.5 16.8 %collective-permute-start.6 = (bf16[2,200,256]{2,1,0:T(8,128)(2,1)S(1)}, bf16[2,200,256]{2,1,0:T(8,128)(2,1)S(1)}, u32[]{:S(2)}, u32[]{:S(2)}) collective-permute-start(bf16[2,200,256]{2,1,0:T(8,128)(2,1)S(1)} %get-tuple-element.305), channel_id=1, source_target_pairs={{0,8},{4,12},{8,0},{12,4},{1,9},{5,13},{9,1},{13,5},{2,10},{6,14},... | collective-permute-start | bytes 614408 | tf_op jit(solution)/shard_map/ppermute | solution.py:273
  21.5 16.7 %collective-permute-start.5 = (bf16[2,200,256]{2,1,0:T(8,128)(2,1)S(1)}, bf16[2,200,256]{2,1,0:T(8,128)(2,1)S(1)}, u32[]{:S(2)}, u32[]{:S(2)}) collective-permute-start(bf16[2,200,256]{2,1,0:T(8,128)(2,1)S(1)} %get-tuple-element.305), channel_id=1, source_target_pairs={{0,4},{4,8},{8,12},{12,0},{1,5},{5,9},{9,13},{13,1},{2,6},{6,10},{... | collective-permute-start | bytes 614408 | tf_op jit(solution)/shard_map/ppermute | solution.py:273
  38.5 8.1 %collective-permute-start.14 = (bf16[2,256,256]{2,1,0:T(8,128)(2,1)S(1)}, bf16[2,256,256]{2,1,0:T(8,128)(2,1)S(1)}, u32[]{:S(2)}, u32[]{:S(2)}) collective-permute-start(bf16[2,256,256]{2,1,0:T(8,128)(2,1)S(1)} %pad_maximum_fusion.9), channel_id=1, source_target_pairs={{0,1},{1,0},{2,3},{3,2},{4,5},{5,4},{6,7},{7,6},{8,9},{9,8},{10,11... | collective-permute-start | bytes 786440 | tf_op jit(solution)/shard_map/ppermute | solution.py:268
  38.9 19.8 %collective-permute-start.8 = (bf16[4,2,200,256]{3,2,1,0:T(8,128)(2,1)S(1)}, bf16[4,2,200,256]{3,2,1,0:T(8,128)(2,1)S(1)}, u32[]{:S(2)}, u32[]{:S(2)}) collective-permute-start(bf16[4,2,200,256]{3,2,1,0:T(8,128)(2,1)S(1)} %pad_maximum_fusion.4.own), channel_id=1, source_target_pairs={{0,2},{2,0},{1,3},{3,1},{4,6},{6,4},{5,7},{7,5},{8,10},{10,8},{9,1... | collective-permute-start | bytes 2457608 | tf_op jit(solution)/shard_map/ppermute | solution.py:268
  39.6 9.5 %collective-permute-start.2 = (bf16[256,1024]{1,0:T(8,128)(2,1)S(1)}, bf16[256,1024]{1,0:T(8,128)(2,1)S(1)}, u32[]{:S(2)}, u32[]{:S(2)}) collective-permute-start(bf16[256,1024]{1,0:T(8,128)(2,1)S(1)} %collective-permute-done.x00.refs_0_), channel_id=1, source_target_pairs={{0,16},{16,0},{1,17},{17,1},{2,18},{18,2},{3,19},{19,3},{4,20},{20... | collective-permute-start | bytes 1572872 | tf_op jit(solution)/shard_map/ppermute | solution.py:268
  41.2 8.1 %collective-permute-start.3 = (bf16[256,1024]{1,0:T(8,128)(2,1)S(1)}, bf16[256,1024]{1,0:T(8,128)(2,1)S(1)}, u32[]{:S(2)}, u32[]{:S(2)}) collective-permute-start(bf16[256,1024]{1,0:T(8,128)(2,1)S(1)} %collective-permute-done.1.x01.refs_1_), channel_id=1, source_target_pairs={{0,16},{16,0},{1,17},{17,1},{2,18},{18,2},{3,19},{19,3},{4,20},{20... | collective-permute-start | bytes 1572872 | tf_op jit(solution)/shard_map/ppermute | solution.py:268
  41.3 24.8 %collective-permute-start.12 = (bf16[336,512]{1,0:T(8,128)(2,1)S(1)}, bf16[336,512]{1,0:T(8,128)(2,1)S(1)}, u32[]{:S(2)}, u32[]{:S(2)}) collective-permute-start(bf16[336,512]{1,0:T(8,128)(2,1)S(1)} %fusion.46), channel_id=1, source_target_pairs={{0,12},{4,0},{8,4},{12,8},{1,13},{5,1},{9,5},{13,9},{2,14},{6,2},{... | collective-permute-start | bytes 1032200 | tf_op jit(solution)/shard_map/ppermute | solution.py:273
  46.7 26.6 %collective-permute-start.11 = (bf16[336,512]{1,0:T(8,128)(2,1)S(1)}, bf16[336,512]{1,0:T(8,128)(2,1)S(1)}, u32[]{:S(2)}, u32[]{:S(2)}) collective-permute-start(bf16[336,512]{1,0:T(8,128)(2,1)S(1)} %fusion.46), channel_id=1, source_target_pairs={{0,8},{4,12},{8,0},{12,4},{1,9},{5,13},{9,1},{13,5},{2,10},{6,14},... | collective-permute-start | bytes 1032200 | tf_op jit(solution)/shard_map/ppermute | solution.py:273
  49.2 24.1 %collective-permute-start.10 = (bf16[336,512]{1,0:T(8,128)(2,1)S(1)}, bf16[336,512]{1,0:T(8,128)(2,1)S(1)}, u32[]{:S(2)}, u32[]{:S(2)}) collective-permute-start(bf16[336,512]{1,0:T(8,128)(2,1)S(1)} %fusion.46), channel_id=1, source_target_pairs={{0,4},{4,8},{8,12},{12,0},{1,5},{5,9},{9,13},{13,1},{2,6},{6,10},{... | collective-permute-start | bytes 1032200 | tf_op jit(solution)/shard_map/ppermute | solution.py:273
  49.3 24.1 %collective-permute-start.15 = (bf16[2,256,256]{2,1,0:T(8,128)(2,1)S(1)}, bf16[2,256,256]{2,1,0:T(8,128)(2,1)S(1)}, u32[]{:S(2)}, u32[]{:S(2)}) collective-permute-start(bf16[2,256,256]{2,1,0:T(8,128)(2,1)S(1)} %pad_maximum_fusion.10), channel_id=1, source_target_pairs={{0,16},{16,0},{1,17},{17,1},{2,18},{18,2},{3,19},{19,3},{4,20},{20... | collective-permute-start | bytes 786440 | tf_op jit(solution)/shard_map/ppermute | solution.py:268
  73.5 11.2 %collective-permute-start.17 = (bf16[256,512]{1,0:T(8,128)(2,1)S(1)}, bf16[256,512]{1,0:T(8,128)(2,1)S(1)}, u32[]{:S(2)}, u32[]{:S(2)}) collective-permute-start(bf16[256,512]{1,0:T(8,128)(2,1)S(1)} %get-tuple-element.173), channel_id=1, source_target_pairs={{0,12},{4,0},{8,4},{12,8},{1,13},{5,1},{9,5},{13,9},{2,14},{6,2},{... | collective-permute-start | bytes 786440 | tf_op jit(solution)/shard_map/ppermute | solution.py:273
  73.6 13.8 %collective-permute-start.16 = (bf16[256,512]{1,0:T(8,128)(2,1)S(1)}, bf16[256,512]{1,0:T(8,128)(2,1)S(1)}, u32[]{:S(2)}, u32[]{:S(2)}) collective-permute-start(bf16[256,512]{1,0:T(8,128)(2,1)S(1)} %get-tuple-element.173), channel_id=1, source_target_pairs={{0,4},{4,8},{8,12},{12,0},{1,5},{5,9},{9,13},{13,1},{2,6},{6,10},{... | collective-permute-start | bytes 786440 | tf_op jit(solution)/shard_map/ppermute | solution.py:273
  75.4 12.1 %collective-permute-start.18 = (bf16[4,72,512]{2,1,0:T(8,128)(2,1)S(1)}, bf16[4,72,512]{2,1,0:T(8,128)(2,1)S(1)}, u32[]{:S(2)}, u32[]{:S(2)}) collective-permute-start(bf16[4,72,512]{2,1,0:T(8,128)(2,1)S(1)} %slice.171.own), channel_id=1, source_target_pairs={{0,2},{2,0},{1,3},{3,1},{4,6},{6,4},{5,7},{7,5},{8,10},{10,8},{9,1... | collective-permute-start | bytes 884744 | tf_op jit(solution)/shard_map/ppermute | solution.py:268
  77.2 29.1 %collective-permute-start.20 = (bf16[4,264,512]{2,1,0:T(8,128)(2,1)S(1)}, bf16[4,264,512]{2,1,0:T(8,128)(2,1)S(1)}, u32[]{:S(2)}, u32[]{:S(2)}) collective-permute-start(bf16[4,264,512]{2,1,0:T(8,128)(2,1)S(1)} %slice.172), channel_id=1, source_target_pairs={{0,2},{2,0},{1,3},{3,1},{4,6},{6,4},{5,7},{7,5},{8,10},{10,8},{9,1... | collective-permute-start | bytes 3244040 | tf_op jit(solution)/shard_map/ppermute | solution.py:268
  89.9 13.8 %collective-permute-start.21 = (bf16[256,512]{1,0:T(8,128)(2,1)S(1)}, bf16[256,512]{1,0:T(8,128)(2,1)S(1)}, u32[]{:S(2)}, u32[]{:S(2)}) collective-permute-start(bf16[256,512]{1,0:T(8,128)(2,1)S(1)} %get-tuple-element.173), channel_id=1, source_target_pairs={{0,8},{4,12},{8,0},{12,4},{1,9},{5,13},{9,1},{13,5},{2,10},{6,14},... | collective-permute-start | bytes 786440 | tf_op jit(solution)/shard_map/ppermute | solution.py:273
  92.4 21.4 %collective-permute-start.23 = (bf16[256,1024]{1,0:T(8,128)(2,1)}, bf16[256,1024]{1,0:T(8,128)(2,1)}, u32[]{:S(2)}, u32[]{:S(2)}) collective-permute-start(bf16[256,1024]{1,0:T(8,128)(2,1)} %add_convert_fusion.2), channel_id=1, source_target_pairs={{0,1},{1,0},{2,3},{3,2},{4,5},{5,4},{6,7},{7,6},{8,9},{9,8},{10,11... | collective-permute-start | bytes 1572872 | tf_op jit(solution)/shard_map/ppermute | solution.py:268
  112.2 24.8 %collective-permute-start.27 = (bf16[4,256,512]{2,1,0:T(8,128)(2,1)S(1)}, bf16[4,256,512]{2,1,0:T(8,128)(2,1)S(1)}, u32[]{:S(2)}, u32[]{:S(2)}) collective-permute-start(bf16[4,256,512]{2,1,0:T(8,128)(2,1)S(1)} %pad_maximum_fusion.3), channel_id=1, source_target_pairs={{0,2},{2,0},{1,3},{3,1},{4,6},{6,4},{5,7},{7,5},{8,10},{10,8},{9,1... | collective-permute-start | bytes 3145736 | tf_op jit(solution)/shard_map/ppermute | solution.py:268
  116.6 13.3 %collective-permute-start.25 = (bf16[256,1024]{1,0:T(8,128)(2,1)S(1)}, bf16[256,1024]{1,0:T(8,128)(2,1)S(1)}, u32[]{:S(2)}, u32[]{:S(2)}) collective-permute-start(bf16[256,1024]{1,0:T(8,128)(2,1)S(1)} %get-tuple-element.178.r0), channel_id=1, source_target_pairs={{0,1},{1,0},{2,3},{3,2},{4,5},{5,4},{6,7},{7,6},{8,9},{9,8},{10,11... | collective-permute-start | bytes 1572872 | tf_op jit(solution)/shard_map/ppermute | solution.py:268
  143.8 13.4 %collective-permute-start.30 = (bf16[256,1024]{1,0:T(8,128)(2,1)S(1)}, bf16[256,1024]{1,0:T(8,128)(2,1)S(1)}, u32[]{:S(2)}, u32[]{:S(2)}) collective-permute-start(bf16[256,1024]{1,0:T(8,128)(2,1)S(1)} %fusion.17), channel_id=1, source_target_pairs={{0,1},{1,0},{2,3},{3,2},{4,5},{5,4},{6,7},{7,6},{8,9},{9,8},{10,11... | collective-permute-start | bytes 1572872 | tf_op jit(solution)/shard_map/ppermute | solution.py:268
  161.0 13.5 %collective-permute-start.32 = (bf16[256,1024]{1,0:T(8,128)(2,1)S(1)}, bf16[256,1024]{1,0:T(8,128)(2,1)S(1)}, u32[]{:S(2)}, u32[]{:S(2)}) collective-permute-start(bf16[256,1024]{1,0:T(8,128)(2,1)S(1)} %get-tuple-element.193.r0), channel_id=1, source_target_pairs={{0,1},{1,0},{2,3},{3,2},{4,5},{5,4},{6,7},{7,6},{8,9},{9,8},{10,11... | collective-permute-start | bytes 1572872 | tf_op jit(solution)/shard_map/ppermute | solution.py:268
  183.5 13.2 %collective-permute-start.36 = (bf16[256,1024]{1,0:T(8,128)(2,1)S(1)}, bf16[256,1024]{1,0:T(8,128)(2,1)S(1)}, u32[]{:S(2)}, u32[]{:S(2)}) collective-permute-start(bf16[256,1024]{1,0:T(8,128)(2,1)S(1)} %add_convert_fusion.1), channel_id=1, source_target_pairs={{0,1},{1,0},{2,3},{3,2},{4,5},{5,4},{6,7},{7,6},{8,9},{9,8},{10,11... | collective-permute-start | bytes 1572872 | tf_op jit(solution)/shard_map/ppermute | solution.py:268
  184.7 10.2 %collective-permute-start.35 = (bf16[256,1024]{1,0:T(8,128)(2,1)S(1)}, bf16[256,1024]{1,0:T(8,128)(2,1)S(1)}, u32[]{:S(2)}, u32[]{:S(2)}) collective-permute-start(bf16[256,1024]{1,0:T(8,128)(2,1)S(1)} %convolution_convert_fusion), channel_id=1, source_target_pairs={{0,16},{16,0},{1,17},{17,1},{2,18},{18,2},{3,19},{19,3},{4,20},{20... | collective-permute-start | bytes 1572872 | tf_op jit(solution)/shard_map/ppermute | solution.py:268
  189.4 24.9 %collective-permute-start.38 = (bf16[4,256,512]{2,1,0:T(8,128)(2,1)S(1)}, bf16[4,256,512]{2,1,0:T(8,128)(2,1)S(1)}, u32[]{:S(2)}, u32[]{:S(2)}) collective-permute-start(bf16[4,256,512]{2,1,0:T(8,128)(2,1)S(1)} %get-tuple-element.207), channel_id=1, source_target_pairs={{0,2},{2,0},{1,3},{3,1},{4,6},{6,4},{5,7},{7,5},{8,10},{10,8},{9,1... | collective-permute-start | bytes 3145736 | tf_op jit(solution)/shard_map/ppermute | solution.py:268
  198.2 16.0 %collective-permute-start.37 = (bf16[256,1024]{1,0:T(8,128)(2,1)S(1)}, bf16[256,1024]{1,0:T(8,128)(2,1)S(1)}, u32[]{:S(2)}, u32[]{:S(2)}) collective-permute-start(bf16[256,1024]{1,0:T(8,128)(2,1)S(1)} %get-tuple-element.204.d0), channel_id=1, source_target_pairs={{0,1},{1,0},{2,3},{3,2},{4,5},{5,4},{6,7},{7,6},{8,9},{9,8},{10,11... | collective-permute-start | bytes 1572872 | tf_op jit(solution)/shard_map/ppermute | solution.py:268
  216.8 24.8 %collective-permute-start.43 = (bf16[4,264,512]{2,1,0:T(8,128)(2,1)S(1)}, bf16[4,264,512]{2,1,0:T(8,128)(2,1)S(1)}, u32[]{:S(2)}, u32[]{:S(2)}) collective-permute-start(bf16[4,264,512]{2,1,0:T(8,128)(2,1)S(1)} %get-tuple-element.221), channel_id=1, source_target_pairs={{0,2},{2,0},{1,3},{3,1},{4,6},{6,4},{5,7},{7,5},{8,10},{10,8},{9,1... | collective-permute-start | bytes 3244040 | tf_op jit(solution)/shard_map/ppermute | solution.py:268
  221.8 23.4 %collective-permute-start.44 = (bf16[256,512]{1,0:T(8,128)(2,1)S(1)}, bf16[256,512]{1,0:T(8,128)(2,1)S(1)}, u32[]{:S(2)}, u32[]{:S(2)}) collective-permute-start(bf16[256,512]{1,0:T(8,128)(2,1)S(1)} %get-tuple-element.216), channel_id=1, source_target_pairs={{0,12},{4,0},{8,4},{12,8},{1,13},{5,1},{9,5},{13,9},{2,14},{6,2},{... | collective-permute-start | bytes 786440 | tf_op jit(solution)/shard_map/ppermute | solution.py:273
  223.8 23.3 %collective-permute-start.45 = (bf16[256,512]{1,0:T(8,128)(2,1)S(1)}, bf16[256,512]{1,0:T(8,128)(2,1)S(1)}, u32[]{:S(2)}, u32[]{:S(2)}) collective-permute-start(bf16[256,512]{1,0:T(8,128)(2,1)S(1)} %get-tuple-element.217), channel_id=1, source_target_pairs={{0,8},{4,12},{8,0},{12,4},{1,9},{5,13},{9,1},{13,5},{2,10},{6,14},... | collective-permute-start | bytes 786440 | tf_op jit(solution)/shard_map/ppermute | solution.py:273
  223.8 24.1 %collective-permute-start.46 = (bf16[256,512]{1,0:T(8,128)(2,1)S(1)}, bf16[256,512]{1,0:T(8,128)(2,1)S(1)}, u32[]{:S(2)}, u32[]{:S(2)}) collective-permute-start(bf16[256,512]{1,0:T(8,128)(2,1)S(1)} %get-tuple-element.218), channel_id=1, source_target_pairs={{0,4},{4,8},{8,12},{12,0},{1,5},{5,9},{9,13},{13,1},{2,6},{6,10},{... | collective-permute-start | bytes 786440 | tf_op jit(solution)/shard_map/ppermute | solution.py:273
  224.2 24.4 %collective-permute-start.41 = (bf16[2,256,256]{2,1,0:T(8,128)(2,1)S(1)}, bf16[2,256,256]{2,1,0:T(8,128)(2,1)S(1)}, u32[]{:S(2)}, u32[]{:S(2)}) collective-permute-start(bf16[2,256,256]{2,1,0:T(8,128)(2,1)S(1)} %pad_maximum_fusion.11), channel_id=1, source_target_pairs={{0,16},{16,0},{1,17},{17,1},{2,18},{18,2},{3,19},{19,3},{4,20},{20... | collective-permute-start | bytes 786440 | tf_op jit(solution)/shard_map/ppermute | solution.py:268
  241.6 21.0 %collective-permute-start.50 = (bf16[2,2,272,256]{3,2,1,0:T(8,128)(2,1)}, bf16[2,2,272,256]{3,2,1,0:T(8,128)(2,1)}, u32[]{:S(2)}, u32[]{:S(2)}) collective-permute-start(bf16[2,2,272,256]{3,2,1,0:T(8,128)(2,1)} %get-tuple-element.227), channel_id=1, source_target_pairs={{0,2},{2,0},{1,3},{3,1},{4,6},{6,4},{5,7},{7,5},{8,10},{10,8},{9,1... | collective-permute-start | bytes 1671176 | tf_op jit(solution)/shard_map/ppermute | solution.py:268
  245.2 14.2 %collective-permute-start.47 = (bf16[264,512]{1,0:T(8,128)(2,1)S(1)}, bf16[264,512]{1,0:T(8,128)(2,1)S(1)}, u32[]{:S(2)}, u32[]{:S(2)}) collective-permute-start(bf16[264,512]{1,0:T(8,128)(2,1)S(1)} %get-tuple-element.229), channel_id=1, source_target_pairs={{0,12},{4,0},{8,4},{12,8},{1,13},{5,1},{9,5},{13,9},{2,14},{6,2},{... | collective-permute-start | bytes 811016 | tf_op jit(solution)/shard_map/ppermute | solution.py:273
  247.8 11.6 %collective-permute-start.48 = (bf16[264,512]{1,0:T(8,128)(2,1)S(1)}, bf16[264,512]{1,0:T(8,128)(2,1)S(1)}, u32[]{:S(2)}, u32[]{:S(2)}) collective-permute-start(bf16[264,512]{1,0:T(8,128)(2,1)S(1)} %get-tuple-element.231), channel_id=1, source_target_pairs={{0,4},{4,8},{8,12},{12,0},{1,5},{5,9},{9,13},{13,1},{2,6},{6,10},{... | collective-permute-start | bytes 811016 | tf_op jit(solution)/shard_map/ppermute | solution.py:273
  260.1 14.5 %collective-permute-start.49 = (bf16[2,2,272,256]{3,2,1,0:T(8,128)(2,1)}, bf16[2,2,272,256]{3,2,1,0:T(8,128)(2,1)}, u32[]{:S(2)}, u32[]{:S(2)}) collective-permute-start(bf16[2,2,272,256]{3,2,1,0:T(8,128)(2,1)} %get-tuple-element.235), channel_id=1, source_target_pairs={{0,2},{2,0},{1,3},{3,1},{4,6},{6,4},{5,7},{7,5},{8,10},{10,8},{9,1... | collective-permute-start | bytes 1671176 | tf_op jit(solution)/shard_map/ppermute | solution.py:268
  260.1 14.4 %collective-permute-start.51 = (bf16[264,512]{1,0:T(8,128)(2,1)}, bf16[264,512]{1,0:T(8,128)(2,1)}, u32[]{:S(2)}, u32[]{:S(2)}) collective-permute-start(bf16[264,512]{1,0:T(8,128)(2,1)} %get-tuple-element.230), channel_id=1, source_target_pairs={{0,8},{4,12},{8,0},{12,4},{1,9},{5,13},{9,1},{13,5},{2,10},{6,14},... | collective-permute-start | bytes 811016 | tf_op jit(solution)/shard_map/ppermute | solution.py:273
  277.2 7.7 %collective-permute-start.53 = (bf16[256,1024]{1,0:T(8,128)(2,1)S(1)}, bf16[256,1024]{1,0:T(8,128)(2,1)S(1)}, u32[]{:S(2)}, u32[]{:S(2)}) collective-permute-start(bf16[256,1024]{1,0:T(8,128)(2,1)S(1)} %fusion.16), channel_id=1, source_target_pairs={{0,16},{16,0},{1,17},{17,1},{2,18},{18,2},{3,19},{19,3},{4,20},{20... | collective-permute-start | bytes 1572872 | tf_op jit(solution)/shard_map/ppermute | solution.py:268
  279.4 15.4 %collective-permute-start.56 = (bf16[2,272,256]{2,1,0:T(8,128)(2,1)S(1)}, bf16[2,272,256]{2,1,0:T(8,128)(2,1)S(1)}, u32[]{:S(2)}, u32[]{:S(2)}) collective-permute-start(bf16[2,272,256]{2,1,0:T(8,128)(2,1)S(1)} %get-tuple-element.238), channel_id=1, source_target_pairs={{0,12},{4,0},{8,4},{12,8},{1,13},{5,1},{9,5},{13,9},{2,14},{6,2},{... | collective-permute-start | bytes 835592 | tf_op jit(solution)/shard_map/ppermute | solution.py:273
  282.2 10.8 %collective-permute-start.52 = (bf16[256,1024]{1,0:T(8,128)(2,1)S(1)}, bf16[256,1024]{1,0:T(8,128)(2,1)S(1)}, u32[]{:S(2)}, u32[]{:S(2)}) collective-permute-start(bf16[256,1024]{1,0:T(8,128)(2,1)S(1)} %pad_maximum_fusion.6), channel_id=1, source_target_pairs={{0,0},{2,16},{16,2},{18,18},{1,1},{3,17},{17,3},{19,19},{4,4},{6,2... | collective-permute-start | bytes 1572872 | tf_op jit(solution)/shard_map/ppermute | solution.py:1051
  285.4 24.2 %collective-permute-start.55 = (bf16[256,1024]{1,0:T(8,128)(2,1)S(1)}, bf16[256,1024]{1,0:T(8,128)(2,1)S(1)}, u32[]{:S(2)}, u32[]{:S(2)}) collective-permute-start(bf16[256,1024]{1,0:T(8,128)(2,1)S(1)} %fusion.15), channel_id=1, source_target_pairs={{0,1},{1,0},{2,3},{3,2},{4,5},{5,4},{6,7},{7,6},{8,9},{9,8},{10,11... | collective-permute-start | bytes 1572872 | tf_op jit(solution)/shard_map/ppermute | solution.py:268
  288.8 20.9 %collective-permute-start.54 = (bf16[256,1024]{1,0:T(8,128)(2,1)S(1)}, bf16[256,1024]{1,0:T(8,128)(2,1)S(1)}, u32[]{:S(2)}, u32[]{:S(2)}) collective-permute-start(bf16[256,1024]{1,0:T(8,128)(2,1)S(1)} %get-tuple-element.255), channel_id=1, source_target_pairs={{0,16},{16,0},{1,17},{17,1},{2,18},{18,2},{3,19},{19,3},{4,20},{20... | collective-permute-start | bytes 1572872 | tf_op jit(solution)/shard_map/ppermute | solution.py:268
  288.8 20.8 %collective-permute-start.57 = (bf16[2,272,256]{2,1,0:T(8,128)(2,1)S(1)}, bf16[2,272,256]{2,1,0:T(8,128)(2,1)S(1)}, u32[]{:S(2)}, u32[]{:S(2)}) collective-permute-start(bf16[2,272,256]{2,1,0:T(8,128)(2,1)S(1)} %get-tuple-element.239), channel_id=1, source_target_pairs={{0,8},{4,12},{8,0},{12,4},{1,9},{5,13},{9,1},{13,5},{2,10},{6,14},... | collective-permute-start | bytes 835592 | tf_op jit(solution)/shard_map/ppermute | solution.py:273
  292.9 16.7 %collective-permute-start.58 = (bf16[2,272,256]{2,1,0:T(8,128)(2,1)S(1)}, bf16[2,272,256]{2,1,0:T(8,128)(2,1)S(1)}, u32[]{:S(2)}, u32[]{:S(2)}) collective-permute-start(bf16[2,272,256]{2,1,0:T(8,128)(2,1)S(1)} %get-tuple-element.240), channel_id=1, source_target_pairs={{0,4},{4,8},{8,12},{12,0},{1,5},{5,9},{9,13},{13,1},{2,6},{6,10},{... | collective-permute-start | bytes 835592 | tf_op jit(solution)/shard_map/ppermute | solution.py:273
  294.8 14.8 %collective-permute-start.59 = (bf16[520,256]{1,0:T(8,128)(2,1)S(1)}, bf16[520,256]{1,0:T(8,128)(2,1)S(1)}, u32[]{:S(2)}, u32[]{:S(2)}) collective-permute-start(bf16[520,256]{1,0:T(8,128)(2,1)S(1)} %get-tuple-element.259), channel_id=1, source_target_pairs={{0,1},{1,0},{2,3},{3,2},{4,5},{5,4},{6,7},{7,6},{8,9},{9,8},{10,11... | collective-permute-start | bytes 798728 | tf_op jit(solution)/shard_map/ppermute | solution.py:268
  310.9 10.5 %collective-permute-start.60 = (bf16[256,1024]{1,0:T(8,128)(2,1)S(1)}, bf16[256,1024]{1,0:T(8,128)(2,1)S(1)}, u32[]{:S(2)}, u32[]{:S(2)}) collective-permute-start(bf16[256,1024]{1,0:T(8,128)(2,1)S(1)} %add_convert_fusion), channel_id=1, source_target_pairs={{0,0},{2,16},{16,2},{18,18},{1,1},{3,17},{17,3},{19,19},{4,4},{6,2... | collective-permute-start | bytes 1572872 | tf_op jit(solution)/shard_map/ppermute | solution.py:1065
  (84 other events, 890.2 us)
where the time goes:
time: 334 us; the launch traced here: 328 us
  waiting for transfers between devices  153 us (46%)
  Pallas kernels  73.8 us (22%)
  starting transfers between devices  68.2 us (20%)
  matrix products  15 us (4%)
  local copies, waits for them, and re-layouts  8.67 us (3%)
  other arithmetic  7.09 us (2%)
    ppermute x42, waiting for transfers between devices, flip(): return lax.ppermute(values, axis_name, PAIR)  84.4 us
    pallas_call x23, Pallas kernels, kernel_call(): pl.pallas_call(kernel, grid_spec=pltpu.PrefetchScalarGridSpec(num_scalar_...  73.8 us
    ppermute x18, waiting for transfers between devices, shift(): lax.ppermute(values, axis_name, [(i, (i + step) % size) for i in range(si...  60.4 us
    ppermute x42, starting transfers between devices, flip(): return lax.ppermute(values, axis_name, PAIR)  39 us
    ppermute x18, starting transfers between devices, shift(): lax.ppermute(values, axis_name, [(i, (i + step) % size) for i in range(si...  16.4 us
  transfers between devices with their start and end apart: 64, of which 27 were waited for; matrix products, arithmetic and copies ran while one was open for 5% of the time, Pallas kernels for 20%

commit v1 on v0

--- a/solution.py
+++ b/solution.py
@@ -262,6 +262,7 @@
 PAIR = ((0, 1), (1, 0))
 MEBIBYTE = 1024 * 1024
 BLOCK = 256
+QUERIES = 512
 
 
 def flip(values, axis_name):
@@ -372,8 +373,8 @@
     value = (total[2 * head_rows :] + bias[head_rows:, 0:1]).astype(BF)
     qkv_ref[0, 2] = value
     key_t = key.T
-    for start in range(0, SEQ, BLOCK):
-        here = slice(start, start + BLOCK)
+    for start in range(0, SEQ, QUERIES):
+        here = slice(start, start + QUERIES)
         scores = matmul(key_t, qkv_ref[0, 0, :, here])
         top = jnp.max(scores, axis=0, keepdims=True)
         weights = jnp.exp(scores - top)
@@ -722,15 +723,16 @@
     )
     ff_got = flip(ff_send, "t")
     attn_got = after(attn_got, x00)
-    cot = lax.ppermute(after(cotangent, x00), ("dp", "u"), swap_cores)
-    x01 = flip(x00, "t")
-    x10, x11 = flip(x00, "dp"), flip(x01, "dp")
+    x10 = flip(x00, "dp")
+    qkv_part = jnp.stack([attn_keep[: qkv_rows + 8], attn_got[: qkv_rows + 8]])
+    cot = lax.ppermute(after(cotangent, qkv_part), ("dp", "u"), swap_cores)
+    x01 = flip(after(x00, qkv_part), "t")
+    x11 = flip(x01, "dp")
     cot = after(cot, x01)
     cot_parts = [cut(cot, quarter ^ j, own_rows, 1) for j in range(4)]
     cot_far = flip(jnp.stack([cot_parts[2], cot_parts[3]]), "t")
     cot_near = flip(jnp.stack([cot_parts[1], cot_far[1]]), "dp")
 
-    qkv_part = jnp.stack([attn_keep[: qkv_rows + 8], attn_got[: qkv_rows + 8]])
     ff_got = after(ff_got, qkv_part)
     qkv_own = jnp.stack(gather_rows(qkv_part))
     attn_both = in_order(chip, attn_keep[qkv_rows + 8 :], attn_got[qkv_rows + 8 :], 1)

time: 334 us -> 332 us (level)
  Pallas kernels: 73.8 us -> 69.9 us
    pallas_call x23, Pallas kernels: 73.8 us -> 69.9 us  [kernel_call(): pl.pallas_call(kernel, grid_spec=pltpu.PrefetchScalarGridSpec(num_scalar_...]
  transfers between devices with their start and end apart: 64 -> 64, of which waited for: 27 -> 27; matrix products, arithmetic and copies ran while one was open for 5% -> 4% of each run, Pallas kernels for 20% -> 19%
where the time goes in v1:
time: 332 us; the launch traced here: 327 us
  waiting for transfers between devices  156 us (47%)
  Pallas kernels  69.9 us (21%)
  starting transfers between devices  68.8 us (21%)
  matrix products  15 us (5%)
  local copies, waits for them, and re-layouts  7.99 us (2%)
  other arithmetic  7.09 us (2%)
    ppermute x42, waiting for transfers between devices, flip(): return lax.ppermute(values, axis_name, PAIR)  84.1 us
    pallas_call x23, Pallas kernels, kernel_call(): pl.pallas_call(kernel, grid_spec=pltpu.PrefetchScalarGridSpec(num_scalar_...  69.9 us
    ppermute x18, waiting for transfers between devices, shift(): lax.ppermute(values, axis_name, [(i, (i + step) % size) for i in range(si...  63.1 us
    ppermute x42, starting transfers between devices, flip(): return lax.ppermute(values, axis_name, PAIR)  38.6 us
    ppermute x18, starting transfers between devices, shift(): lax.ppermute(values, axis_name, [(i, (i + step) % size) for i in range(si...  17.1 us
  transfers between devices with their start and end apart: 64, of which 27 were waited for; matrix products, arithmetic and copies ran while one was open for 4% of the time, Pallas kernels for 19%

profile of v1, /device:TPU:1, one launch (start us, length us, event | category | flops | bytes accessed | tf_op | source)
XLA Modules:
  0.0 327.0 jit_solution(12934586610376959749)
XLA Ops:
  0.7 4.7 %collective-permute-start = (bf16[256,1024]{1,0:T(8,128)(2,1)}, bf16[256,1024]{1,0:T(8,128)(2,1)S(1)}, u32[]{:S(2)}, u32[]{:S(2)}) collective-permute-start(bf16[256,1024]{1,0:T(8,128)(2,1)} %param.14), channel_id=1, source_target_pairs={{0,0},{2,16},{16,2},{18,18},{1,1},{3,17},{17,3},{19,19},{4,4},{6,2... | collective-permute-start | bytes 1572872 | tf_op jit(solution)/shard_map/ppermute | solution.py:700
  6.0 2.7 prepare_attn.1
  9.9 2.7 prepare_ff.1
  15.2 2.7 collective-permute-start.13
  18.0 3.4 %collective-permute-start.7 = (bf16[2,200,256]{2,1,0:T(8,128)(2,1)S(1)}, bf16[2,200,256]{2,1,0:T(8,128)(2,1)S(1)}, u32[]{:S(2)}, u32[]{:S(2)}) collective-permute-start(bf16[2,200,256]{2,1,0:T(8,128)(2,1)S(1)} %get-tuple-element.307), channel_id=1, source_target_pairs={{0,12},{4,0},{8,4},{12,8},{1,13},{5,1},{9,5},{13,9},{2,14},{6,2},{... | collective-permute-start | bytes 614408 | tf_op jit(solution)/shard_map/ppermute | solution.py:274
  23.4 2.9 collective-permute-done.7
  26.3 10.8 %collective-permute-done.6 = bf16[2,200,256]{2,1,0:T(8,128)(2,1)S(1)} collective-permute-done((bf16[2,200,256]{2,1,0:T(8,128)(2,1)S(1)}, bf16[2,200,256]{2,1,0:T(8,128)(2,1)S(1)}, u32[]{:S(2)}, u32[]{:S(2)}) %collective-permute-start.6) | collective-permute-done | bytes 204832 | tf_op jit(solution)/shard_map/ppermute | solution.py:274
  40.0 5.4 %collective-permute-done.14 = bf16[2,256,256]{2,1,0:T(8,128)(2,1)S(1)} collective-permute-done((bf16[2,256,256]{2,1,0:T(8,128)(2,1)S(1)}, bf16[2,256,256]{2,1,0:T(8,128)(2,1)S(1)}, u32[]{:S(2)}, u32[]{:S(2)}) %collective-permute-start.14) | collective-permute-done | bytes 262176 | tf_op jit(solution)/shard_map/ppermute | solution.py:269
  45.4 2.6 collective-permute-start.11
  49.4 8.1 %collective-permute-done.8.far = bf16[4,2,200,256]{3,2,1,0:T(8,128)(2,1)S(1)} collective-permute-done((bf16[4,2,200,256]{3,2,1,0:T(8,128)(2,1)S(1)}, bf16[4,2,200,256]{3,2,1,0:T(8,128)(2,1)S(1)}, u32[]{:S(2)}, u32[]{:S(2)}) %collective-permute-start.8) | collective-permute-done | bytes 819232 | tf_op jit(solution)/shard_map/ppermute | solution.py:269
  57.5 5.5 %attend.2 = (bf16[2,3,64,1024]{3,2,1,0:T(8,128)(2,1)S(1)}, f32[2,64,1024]{2,1,0:T(8,128)S(1)}, f32[2,1,1024]{2,1,0:T(1,128)S(1)}, bf16[2,192,256]{2,1,0:T(8,128)...) custom-call(s32[6]{0:T(128)S(1)} %copy-done.44, ...), custom_call_target="tpu_custom_call" | custom-call | flops 10000000000 | bytes 100000000 | tf_op jit(solution)/shard_map/attend/pallas_call | solution.py:302
  63.1 9.1 %collective-permute-done.11 = bf16[336,512]{1,0:T(8,128)(2,1)S(1)} collective-permute-done((bf16[336,512]{1,0:T(8,128)(2,1)S(1)}, bf16[336,512]{1,0:T(8,128)(2,1)S(1)}, u32[]{:S(2)}, u32[]{:S(2)}) %collective-permute-start.11) | collective-permute-done | bytes 344096 | tf_op jit(solution)/shard_map/ppermute | solution.py:274
  75.9 5.5 %attend.3 = (bf16[2,3,64,1024]{3,2,1,0:T(8,128)(2,1)S(1)}, f32[2,64,1024]{2,1,0:T(8,128)S(1)}, f32[2,1,1024]{2,1,0:T(1,128)S(1)}, bf16[2,192,256]{2,1,0:T(8,128)...) custom-call(s32[6]{0:T(128)S(1)} %copy-done.44, ...), custom_call_target="tpu_custom_call" | custom-call | flops 10000000000 | bytes 100000000 | tf_op jit(solution)/shard_map/attend/pallas_call | solution.py:302
  81.5 4.5 %collective-permute-done.16 = bf16[256,512]{1,0:T(8,128)(2,1)S(1)} collective-permute-done((bf16[256,512]{1,0:T(8,128)(2,1)S(1)}, bf16[256,512]{1,0:T(8,128)(2,1)S(1)}, u32[]{:S(2)}, u32[]{:S(2)}) %collective-permute-start.16) | collective-permute-done | bytes 262176 | tf_op jit(solution)/shard_map/ppermute | solution.py:274
  92.2 10.3 %collective-permute-done.21 = bf16[256,512]{1,0:T(8,128)(2,1)S(1)} collective-permute-done((bf16[256,512]{1,0:T(8,128)(2,1)S(1)}, bf16[256,512]{1,0:T(8,128)(2,1)S(1)}, u32[]{:S(2)}, u32[]{:S(2)}) %collective-permute-start.21) | collective-permute-done | bytes 262176 | tf_op jit(solution)/shard_map/ppermute | solution.py:274
  102.5 2.3 collective-permute-done.20
  104.8 1.7 out_near.1
  106.6 2.2 collective-permute-start.22
  112.4 2.5 norm1.1
  118.3 10.2 %collective-permute-done.25.r2 = bf16[256,1024]{1,0:T(8,128)(2,1)S(1)} collective-permute-done((bf16[256,1024]{1,0:T(8,128)(2,1)S(1)}, bf16[256,1024]{1,0:T(8,128)(2,1)S(1)}, u32[]{:S(2)}, u32[]{:S(2)}) %collective-permute-start.25) | collective-permute-done | bytes 524320 | tf_op jit(solution)/shard_map/ppermute | solution.py:269
  129.6 6.1 %collective-permute-done.27 = bf16[4,256,512]{2,1,0:T(8,128)(2,1)S(1)} collective-permute-done((bf16[4,256,512]{2,1,0:T(8,128)(2,1)S(1)}, bf16[4,256,512]{2,1,0:T(8,128)(2,1)S(1)}, u32[]{:S(2)}, u32[]{:S(2)}) %collective-permute-start.27) | collective-permute-done | bytes 1048608 | tf_op jit(solution)/shard_map/ppermute | solution.py:269
  145.5 10.3 %collective-permute-done.30.got = bf16[256,1024]{1,0:T(8,128)(2,1)S(1)} collective-permute-done((bf16[256,1024]{1,0:T(8,128)(2,1)S(1)}, bf16[256,1024]{1,0:T(8,128)(2,1)S(1)}, u32[]{:S(2)}, u32[]{:S(2)}) %collective-permute-start.30) | collective-permute-done | bytes 524320 | tf_op jit(solution)/shard_map/ppermute | solution.py:269
  155.8 2.8 norm2.1
  161.2 1.8 fusion.5.left_near
  162.9 10.2 %collective-permute-done.32.r2 = bf16[256,1024]{1,0:T(8,128)(2,1)S(1)} collective-permute-done((bf16[256,1024]{1,0:T(8,128)(2,1)S(1)}, bf16[256,1024]{1,0:T(8,128)(2,1)S(1)}, u32[]{:S(2)}, u32[]{:S(2)}) %collective-permute-start.32) | collective-permute-done | bytes 524320 | tf_op jit(solution)/shard_map/ppermute | solution.py:269
  175.5 1.8 fusion.11.left_far
  184.0 4.0 %weight_grad.3 = (bf16[4,256,512]{2,1,0:T(8,128)(2,1)S(1)}, bf16[4,256,512]{2,1,0:T(8,128)(2,1)S(1)}) custom-call(s32[6]{0:T(128)S(1)} %copy-done.44, bf16[512,1024]{1,0:T(8,128)(2,1)S(1)} %get-tuple-element.207.left_near, bf16[512,1024]{1,0:T(8,128)(2,1)S(1)} %get-tuple-element.208.left_far, bf16[256,1024]{1,0:T(8,128)(2,1)S(1)} %get-tuple-element.195.r0, ...), custom_call_target="tpu_custom_call" | custom-call | flops 10000000000 | bytes 100000000 | tf_op jit(solution)/shard_map/weight_grad/pallas_call | solution.py:302
  189.6 4.0 %weight_grad.2 = (bf16[4,264,512]{2,1,0:T(8,128)(2,1)S(1)}, bf16[4,264,512]{2,1,0:T(8,128)(2,1)S(1)}) custom-call(s32[6]{0:T(128)S(1)} %copy-done.44, bf16[512,1024]{1,0:T(8,128)(2,1)S(1)} %fusion.5.left_near, bf16[512,1024]{1,0:T(8,128)(2,1)S(1)} %fusion.11.left_far, bf16[256,1024]{1,0:T(8,128)(2,1)S(1)} %get-tuple-element.180.r0, ...), custom_call_target="tpu_custom_call" | custom-call | flops 10000000000 | bytes 100000000 | tf_op jit(solution)/shard_map/weight_grad/pallas_call | solution.py:302
  193.6 1.8 collective-permute-done.36.got
  198.2 14.7 %collective-permute-done.38.got = bf16[4,256,512]{2,1,0:T(8,128)(2,1)S(1)} collective-permute-done((bf16[4,256,512]{2,1,0:T(8,128)(2,1)S(1)}, bf16[4,256,512]{2,1,0:T(8,128)(2,1)S(1)}, u32[]{:S(2)}, u32[]{:S(2)}) %collective-permute-start.38) | collective-permute-done | bytes 1048608 | tf_op jit(solution)/shard_map/ppermute | solution.py:269
  217.0 1.9 out_back.1
  220.5 1.9 collective-permute-start.44
  224.4 10.3 %attend_back.2 = (bf16[2,192,1024]{2,1,0:T(8,128)(2,1)S(1)}, bf16[2,2,272,256]{3,2,1,0:T(8,128)(2,1)S(1)}, bf16[2,2,272,256]{3,2,1,0:T(8,128)(2,1)}) custom-call(s32[6]{0:T(128)S(1)} %copy-done.44, bf16[2,3,64,1024]{3,2,1,0:T(8,128)(2,1)S(1)} %copy-done.48, bf16[4,64,1024]{2,1,0:T(8,128)(2,1)S(1)} %get-tuple-element.234.grad_ref, ...), custom_call_target="tpu_custom_call" | custom-call | flops 10000000000 | bytes 100000000 | tf_op jit(solution)/shard_map/attend_back/pallas_call | solution.py:302
  234.7 5.5 %collective-permute-done.43.got = bf16[4,264,512]{2,1,0:T(8,128)(2,1)S(1)} collective-permute-done((bf16[4,264,512]{2,1,0:T(8,128)(2,1)S(1)}, bf16[4,264,512]{2,1,0:T(8,128)(2,1)S(1)}, u32[]{:S(2)}, u32[]{:S(2)}) %collective-permute-start.43) | collective-permute-done | bytes 1081376 | tf_op jit(solution)/shard_map/ppermute | solution.py:269
  243.9 1.9 collective-permute-start.47
  247.2 10.0 %attend_back.3 = (bf16[2,192,1024]{2,1,0:T(8,128)(2,1)S(1)}, bf16[2,2,272,256]{3,2,1,0:T(8,128)(2,1)S(1)}, bf16[2,2,272,256]{3,2,1,0:T(8,128)(2,1)}) custom-call(s32[6]{0:T(128)S(1)} %copy-done.44, bf16[2,3,64,1024]{3,2,1,0:T(8,128)(2,1)S(1)} %copy-done.46, bf16[4,64,1024]{2,1,0:T(8,128)(2,1)S(1)} %get-tuple-element.234.grad_ref, ...), custom_call_target="tpu_custom_call" | custom-call | flops 10000000000 | bytes 100000000 | tf_op jit(solution)/shard_map/attend_back/pallas_call | solution.py:302
  261.3 12.0 %collective-permute-done.51.refs_6_ = bf16[264,512]{1,0:T(8,128)(2,1)} collective-permute-done((bf16[264,512]{1,0:T(8,128)(2,1)}, bf16[264,512]{1,0:T(8,128)(2,1)}, u32[]{:S(2)}, u32[]{:S(2)}) %collective-permute-start.51) | collective-permute-done | bytes 270368 | tf_op jit(solution)/shard_map/ppermute | solution.py:274
  273.2 2.1 tail_sum.1
  278.1 2.7 collective-permute-start.56
  280.8 2.7 collective-permute-start.52
  285.4 2.0 input_near.1
  287.5 4.1 %collective-permute-done.52 = bf16[256,1024]{1,0:T(8,128)(2,1)S(1)} collective-permute-done((bf16[256,1024]{1,0:T(8,128)(2,1)S(1)}, bf16[256,1024]{1,0:T(8,128)(2,1)S(1)}, u32[]{:S(2)}, u32[]{:S(2)}) %collective-permute-start.52) | collective-permute-done | bytes 524320 | tf_op jit(solution)/shard_map/ppermute | solution.py:1053
  291.6 1.8 last_ff.1
  294.7 13.5 %collective-permute-done.57.refs_1_ = bf16[2,272,256]{2,1,0:T(8,128)(2,1)S(1)} collective-permute-done((bf16[2,272,256]{2,1,0:T(8,128)(2,1)S(1)}, bf16[2,272,256]{2,1,0:T(8,128)(2,1)S(1)}, u32[]{:S(2)}, u32[]{:S(2)}) %collective-permute-start.57) | collective-permute-done | bytes 278560 | tf_op jit(solution)/shard_map/ppermute | solution.py:274
  309.6 3.0 collective-permute-start.60
  315.5 4.5 %collective-permute-done.60 = bf16[256,1024]{1,0:T(8,128)(2,1)S(1)} collective-permute-done((bf16[256,1024]{1,0:T(8,128)(2,1)S(1)}, bf16[256,1024]{1,0:T(8,128)(2,1)S(1)}, u32[]{:S(2)}, u32[]{:S(2)}) %collective-permute-start.60) | collective-permute-done | bytes 524320 | tf_op jit(solution)/shard_map/ppermute | solution.py:1067
  321.3 2.1 last_ff_out.1
  323.4 1.8 last.1
  (298 shorter events, 83.7 us)
Async XLA Ops:
  0.7 13.1 %collective-permute-start = (bf16[256,1024]{1,0:T(8,128)(2,1)}, bf16[256,1024]{1,0:T(8,128)(2,1)S(1)}, u32[]{:S(2)}, u32[]{:S(2)}) collective-permute-start(bf16[256,1024]{1,0:T(8,128)(2,1)} %param.14), channel_id=1, source_target_pairs={{0,0},{2,16},{16,2},{18,18},{1,1},{3,17},{17,3},{19,19},{4,4},{6,2... | collective-permute-start | bytes 1572872 | tf_op jit(solution)/shard_map/ppermute | solution.py:700
  12.6 8.7 %collective-permute-start.9 = (bf16[512,256]{1,0:T(8,128)(2,1)}, bf16[512,256]{1,0:T(8,128)(2,1)S(1)}, u32[]{:S(2)}, u32[]{:S(2)}) collective-permute-start(bf16[512,256]{1,0:T(8,128)(2,1)} %get-tuple-element.154), channel_id=1, source_target_pairs={{0,1},{1,0},{2,3},{3,2},{4,5},{5,4},{6,7},{7,6},{8,9},{9,8},{10,11... | collective-permute-start | bytes 786440 | tf_op jit(solution)/shard_map/ppermute | solution.py:269
  13.8 23.3 %collective-permute-start.2 = (bf16[256,1024]{1,0:T(8,128)(2,1)S(1)}, bf16[256,1024]{1,0:T(8,128)(2,1)S(1)}, u32[]{:S(2)}, u32[]{:S(2)}) collective-permute-start(bf16[256,1024]{1,0:T(8,128)(2,1)S(1)} %collective-permute-done.x00.refs_0_), channel_id=1, source_target_pairs={{0,1},{1,0},{2,3},{3,2},{4,5},{5,4},{6,7},{7,6},{8,9},{9,8},{10,11... | collective-permute-start | bytes 1572872 | tf_op jit(solution)/shard_map/ppermute | solution.py:269
  15.2 22.0 %collective-permute-start.13 = (bf16[256,1024]{1,0:T(8,128)(2,1)S(1)}, bf16[256,1024]{1,0:T(8,128)(2,1)S(1)}, u32[]{:S(2)}, u32[]{:S(2)}) collective-permute-start(bf16[256,1024]{1,0:T(8,128)(2,1)S(1)} %copy-done.69), channel_id=1, source_target_pairs={{0,0},{2,16},{16,2},{18,18},{1,1},{3,17},{17,3},{19,19},{4,4},{6,2... | collective-permute-start | bytes 1572872 | tf_op jit(solution)/shard_map/ppermute | solution.py:728
  18.0 8.3 %collective-permute-start.7 = (bf16[2,200,256]{2,1,0:T(8,128)(2,1)S(1)}, bf16[2,200,256]{2,1,0:T(8,128)(2,1)S(1)}, u32[]{:S(2)}, u32[]{:S(2)}) collective-permute-start(bf16[2,200,256]{2,1,0:T(8,128)(2,1)S(1)} %get-tuple-element.307), channel_id=1, source_target_pairs={{0,12},{4,0},{8,4},{12,8},{1,13},{5,1},{9,5},{13,9},{2,14},{6,2},{... | collective-permute-start | bytes 614408 | tf_op jit(solution)/shard_map/ppermute | solution.py:274
  21.3 15.7 %collective-permute-start.6 = (bf16[2,200,256]{2,1,0:T(8,128)(2,1)S(1)}, bf16[2,200,256]{2,1,0:T(8,128)(2,1)S(1)}, u32[]{:S(2)}, u32[]{:S(2)}) collective-permute-start(bf16[2,200,256]{2,1,0:T(8,128)(2,1)S(1)} %get-tuple-element.307), channel_id=1, source_target_pairs={{0,8},{4,12},{8,0},{12,4},{1,9},{5,13},{9,1},{13,5},{2,10},{6,14},... | collective-permute-start | bytes 614408 | tf_op jit(solution)/shard_map/ppermute | solution.py:274
  21.3 15.7 %collective-permute-start.5 = (bf16[2,200,256]{2,1,0:T(8,128)(2,1)S(1)}, bf16[2,200,256]{2,1,0:T(8,128)(2,1)S(1)}, u32[]{:S(2)}, u32[]{:S(2)}) collective-permute-start(bf16[2,200,256]{2,1,0:T(8,128)(2,1)S(1)} %get-tuple-element.307), channel_id=1, source_target_pairs={{0,4},{4,8},{8,12},{12,0},{1,5},{5,9},{9,13},{13,1},{2,6},{6,10},{... | collective-permute-start | bytes 614408 | tf_op jit(solution)/shard_map/ppermute | solution.py:274
  37.3 8.1 %collective-permute-start.14 = (bf16[2,256,256]{2,1,0:T(8,128)(2,1)S(1)}, bf16[2,256,256]{2,1,0:T(8,128)(2,1)S(1)}, u32[]{:S(2)}, u32[]{:S(2)}) collective-permute-start(bf16[2,256,256]{2,1,0:T(8,128)(2,1)S(1)} %pad_maximum_fusion.9), channel_id=1, source_target_pairs={{0,1},{1,0},{2,3},{3,2},{4,5},{5,4},{6,7},{7,6},{8,9},{9,8},{10,11... | collective-permute-start | bytes 786440 | tf_op jit(solution)/shard_map/ppermute | solution.py:269
  37.7 19.8 %collective-permute-start.8 = (bf16[4,2,200,256]{3,2,1,0:T(8,128)(2,1)S(1)}, bf16[4,2,200,256]{3,2,1,0:T(8,128)(2,1)S(1)}, u32[]{:S(2)}, u32[]{:S(2)}) collective-permute-start(bf16[4,2,200,256]{3,2,1,0:T(8,128)(2,1)S(1)} %pad_maximum_fusion.4.own), channel_id=1, source_target_pairs={{0,2},{2,0},{1,3},{3,1},{4,6},{6,4},{5,7},{7,5},{8,10},{10,8},{9,1... | collective-permute-start | bytes 2457608 | tf_op jit(solution)/shard_map/ppermute | solution.py:269
  38.4 9.7 %collective-permute-start.3 = (bf16[256,1024]{1,0:T(8,128)(2,1)S(1)}, bf16[256,1024]{1,0:T(8,128)(2,1)S(1)}, u32[]{:S(2)}, u32[]{:S(2)}) collective-permute-start(bf16[256,1024]{1,0:T(8,128)(2,1)S(1)} %collective-permute-done.x00.refs_0_), channel_id=1, source_target_pairs={{0,16},{16,0},{1,17},{17,1},{2,18},{18,2},{3,19},{19,3},{4,20},{20... | collective-permute-start | bytes 1572872 | tf_op jit(solution)/shard_map/ppermute | solution.py:269
  39.8 8.4 %collective-permute-start.4 = (bf16[256,1024]{1,0:T(8,128)(2,1)S(1)}, bf16[256,1024]{1,0:T(8,128)(2,1)S(1)}, u32[]{:S(2)}, u32[]{:S(2)}) collective-permute-start(bf16[256,1024]{1,0:T(8,128)(2,1)S(1)} %collective-permute-done.2.x01.refs_1_), channel_id=1, source_target_pairs={{0,16},{16,0},{1,17},{17,1},{2,18},{18,2},{3,19},{19,3},{4,20},{20... | collective-permute-start | bytes 1572872 | tf_op jit(solution)/shard_map/ppermute | solution.py:269
  39.9 23.1 %collective-permute-start.12 = (bf16[336,512]{1,0:T(8,128)(2,1)S(1)}, bf16[336,512]{1,0:T(8,128)(2,1)S(1)}, u32[]{:S(2)}, u32[]{:S(2)}) collective-permute-start(bf16[336,512]{1,0:T(8,128)(2,1)S(1)} %fusion.46), channel_id=1, source_target_pairs={{0,12},{4,0},{8,4},{12,8},{1,13},{5,1},{9,5},{13,9},{2,14},{6,2},{... | collective-permute-start | bytes 1032200 | tf_op jit(solution)/shard_map/ppermute | solution.py:274
  45.4 26.7 %collective-permute-start.11 = (bf16[336,512]{1,0:T(8,128)(2,1)S(1)}, bf16[336,512]{1,0:T(8,128)(2,1)S(1)}, u32[]{:S(2)}, u32[]{:S(2)}) collective-permute-start(bf16[336,512]{1,0:T(8,128)(2,1)S(1)} %fusion.46), channel_id=1, source_target_pairs={{0,8},{4,12},{8,0},{12,4},{1,9},{5,13},{9,1},{13,5},{2,10},{6,14},... | collective-permute-start | bytes 1032200 | tf_op jit(solution)/shard_map/ppermute | solution.py:274
  48.1 24.0 %collective-permute-start.10 = (bf16[336,512]{1,0:T(8,128)(2,1)S(1)}, bf16[336,512]{1,0:T(8,128)(2,1)S(1)}, u32[]{:S(2)}, u32[]{:S(2)}) collective-permute-start(bf16[336,512]{1,0:T(8,128)(2,1)S(1)} %fusion.46), channel_id=1, source_target_pairs={{0,4},{4,8},{8,12},{12,0},{1,5},{5,9},{9,13},{13,1},{2,6},{6,10},{... | collective-permute-start | bytes 1032200 | tf_op jit(solution)/shard_map/ppermute | solution.py:274
  48.2 24.0 %collective-permute-start.15 = (bf16[2,256,256]{2,1,0:T(8,128)(2,1)S(1)}, bf16[2,256,256]{2,1,0:T(8,128)(2,1)S(1)}, u32[]{:S(2)}, u32[]{:S(2)}) collective-permute-start(bf16[2,256,256]{2,1,0:T(8,128)(2,1)S(1)} %pad_maximum_fusion.10), channel_id=1, source_target_pairs={{0,16},{16,0},{1,17},{17,1},{2,18},{18,2},{3,19},{19,3},{4,20},{20... | collective-permute-start | bytes 786440 | tf_op jit(solution)/shard_map/ppermute | solution.py:269
  72.4 9.1 %collective-permute-start.17 = (bf16[256,512]{1,0:T(8,128)(2,1)S(1)}, bf16[256,512]{1,0:T(8,128)(2,1)S(1)}, u32[]{:S(2)}, u32[]{:S(2)}) collective-permute-start(bf16[256,512]{1,0:T(8,128)(2,1)S(1)} %get-tuple-element.175), channel_id=1, source_target_pairs={{0,12},{4,0},{8,4},{12,8},{1,13},{5,1},{9,5},{13,9},{2,14},{6,2},{... | collective-permute-start | bytes 786440 | tf_op jit(solution)/shard_map/ppermute | solution.py:274
  72.4 13.6 %collective-permute-start.16 = (bf16[256,512]{1,0:T(8,128)(2,1)S(1)}, bf16[256,512]{1,0:T(8,128)(2,1)S(1)}, u32[]{:S(2)}, u32[]{:S(2)}) collective-permute-start(bf16[256,512]{1,0:T(8,128)(2,1)S(1)} %get-tuple-element.175), channel_id=1, source_target_pairs={{0,4},{4,8},{8,12},{12,0},{1,5},{5,9},{9,13},{13,1},{2,6},{6,10},{... | collective-permute-start | bytes 786440 | tf_op jit(solution)/shard_map/ppermute | solution.py:274
  74.2 11.8 %collective-permute-start.18 = (bf16[4,72,512]{2,1,0:T(8,128)(2,1)S(1)}, bf16[4,72,512]{2,1,0:T(8,128)(2,1)S(1)}, u32[]{:S(2)}, u32[]{:S(2)}) collective-permute-start(bf16[4,72,512]{2,1,0:T(8,128)(2,1)S(1)} %slice.171.own), channel_id=1, source_target_pairs={{0,2},{2,0},{1,3},{3,1},{4,6},{6,4},{5,7},{7,5},{8,10},{10,8},{9,1... | collective-permute-start | bytes 884744 | tf_op jit(solution)/shard_map/ppermute | solution.py:269
  75.8 29.0 %collective-permute-start.20 = (bf16[4,264,512]{2,1,0:T(8,128)(2,1)S(1)}, bf16[4,264,512]{2,1,0:T(8,128)(2,1)S(1)}, u32[]{:S(2)}, u32[]{:S(2)}) collective-permute-start(bf16[4,264,512]{2,1,0:T(8,128)(2,1)S(1)} %slice.172), channel_id=1, source_target_pairs={{0,2},{2,0},{1,3},{3,1},{4,6},{6,4},{5,7},{7,5},{8,10},{10,8},{9,1... | collective-permute-start | bytes 3244040 | tf_op jit(solution)/shard_map/ppermute | solution.py:269
  88.5 14.0 %collective-permute-start.21 = (bf16[256,512]{1,0:T(8,128)(2,1)S(1)}, bf16[256,512]{1,0:T(8,128)(2,1)S(1)}, u32[]{:S(2)}, u32[]{:S(2)}) collective-permute-start(bf16[256,512]{1,0:T(8,128)(2,1)S(1)} %get-tuple-element.175), channel_id=1, source_target_pairs={{0,8},{4,12},{8,0},{12,4},{1,9},{5,13},{9,1},{13,5},{2,10},{6,14},... | collective-permute-start | bytes 786440 | tf_op jit(solution)/shard_map/ppermute | solution.py:274
  91.0 21.4 %collective-permute-start.23 = (bf16[256,1024]{1,0:T(8,128)(2,1)}, bf16[256,1024]{1,0:T(8,128)(2,1)}, u32[]{:S(2)}, u32[]{:S(2)}) collective-permute-start(bf16[256,1024]{1,0:T(8,128)(2,1)} %add_convert_fusion.2), channel_id=1, source_target_pairs={{0,1},{1,0},{2,3},{3,2},{4,5},{5,4},{6,7},{7,6},{8,9},{9,8},{10,11... | collective-permute-start | bytes 1572872 | tf_op jit(solution)/shard_map/ppermute | solution.py:269
  110.9 24.8 %collective-permute-start.27 = (bf16[4,256,512]{2,1,0:T(8,128)(2,1)S(1)}, bf16[4,256,512]{2,1,0:T(8,128)(2,1)S(1)}, u32[]{:S(2)}, u32[]{:S(2)}) collective-permute-start(bf16[4,256,512]{2,1,0:T(8,128)(2,1)S(1)} %pad_maximum_fusion.3), channel_id=1, source_target_pairs={{0,2},{2,0},{1,3},{3,1},{4,6},{6,4},{5,7},{7,5},{8,10},{10,8},{9,1... | collective-permute-start | bytes 3145736 | tf_op jit(solution)/shard_map/ppermute | solution.py:269
  115.3 13.3 %collective-permute-start.25 = (bf16[256,1024]{1,0:T(8,128)(2,1)S(1)}, bf16[256,1024]{1,0:T(8,128)(2,1)S(1)}, u32[]{:S(2)}, u32[]{:S(2)}) collective-permute-start(bf16[256,1024]{1,0:T(8,128)(2,1)S(1)} %get-tuple-element.180.r0), channel_id=1, source_target_pairs={{0,1},{1,0},{2,3},{3,2},{4,5},{5,4},{6,7},{7,6},{8,9},{9,8},{10,11... | collective-permute-start | bytes 1572872 | tf_op jit(solution)/shard_map/ppermute | solution.py:269
  142.5 13.4 %collective-permute-start.30 = (bf16[256,1024]{1,0:T(8,128)(2,1)S(1)}, bf16[256,1024]{1,0:T(8,128)(2,1)S(1)}, u32[]{:S(2)}, u32[]{:S(2)}) collective-permute-start(bf16[256,1024]{1,0:T(8,128)(2,1)S(1)} %fusion.17), channel_id=1, source_target_pairs={{0,1},{1,0},{2,3},{3,2},{4,5},{5,4},{6,7},{7,6},{8,9},{9,8},{10,11... | collective-permute-start | bytes 1572872 | tf_op jit(solution)/shard_map/ppermute | solution.py:269
  159.6 13.5 %collective-permute-start.32 = (bf16[256,1024]{1,0:T(8,128)(2,1)S(1)}, bf16[256,1024]{1,0:T(8,128)(2,1)S(1)}, u32[]{:S(2)}, u32[]{:S(2)}) collective-permute-start(bf16[256,1024]{1,0:T(8,128)(2,1)S(1)} %get-tuple-element.195.r0), channel_id=1, source_target_pairs={{0,1},{1,0},{2,3},{3,2},{4,5},{5,4},{6,7},{7,6},{8,9},{9,8},{10,11... | collective-permute-start | bytes 1572872 | tf_op jit(solution)/shard_map/ppermute | solution.py:269
  182.1 13.2 %collective-permute-start.36 = (bf16[256,1024]{1,0:T(8,128)(2,1)S(1)}, bf16[256,1024]{1,0:T(8,128)(2,1)S(1)}, u32[]{:S(2)}, u32[]{:S(2)}) collective-permute-start(bf16[256,1024]{1,0:T(8,128)(2,1)S(1)} %add_convert_fusion.1), channel_id=1, source_target_pairs={{0,1},{1,0},{2,3},{3,2},{4,5},{5,4},{6,7},{7,6},{8,9},{9,8},{10,11... | collective-permute-start | bytes 1572872 | tf_op jit(solution)/shard_map/ppermute | solution.py:269
  183.4 10.2 %collective-permute-start.35 = (bf16[256,1024]{1,0:T(8,128)(2,1)S(1)}, bf16[256,1024]{1,0:T(8,128)(2,1)S(1)}, u32[]{:S(2)}, u32[]{:S(2)}) collective-permute-start(bf16[256,1024]{1,0:T(8,128)(2,1)S(1)} %convolution_convert_fusion), channel_id=1, source_target_pairs={{0,16},{16,0},{1,17},{17,1},{2,18},{18,2},{3,19},{19,3},{4,20},{20... | collective-permute-start | bytes 1572872 | tf_op jit(solution)/shard_map/ppermute | solution.py:269
  188.0 24.9 %collective-permute-start.38 = (bf16[4,256,512]{2,1,0:T(8,128)(2,1)S(1)}, bf16[4,256,512]{2,1,0:T(8,128)(2,1)S(1)}, u32[]{:S(2)}, u32[]{:S(2)}) collective-permute-start(bf16[4,256,512]{2,1,0:T(8,128)(2,1)S(1)} %get-tuple-element.209), channel_id=1, source_target_pairs={{0,2},{2,0},{1,3},{3,1},{4,6},{6,4},{5,7},{7,5},{8,10},{10,8},{9,1... | collective-permute-start | bytes 3145736 | tf_op jit(solution)/shard_map/ppermute | solution.py:269
  196.9 16.0 %collective-permute-start.37 = (bf16[256,1024]{1,0:T(8,128)(2,1)S(1)}, bf16[256,1024]{1,0:T(8,128)(2,1)S(1)}, u32[]{:S(2)}, u32[]{:S(2)}) collective-permute-start(bf16[256,1024]{1,0:T(8,128)(2,1)S(1)} %get-tuple-element.206.d0), channel_id=1, source_target_pairs={{0,1},{1,0},{2,3},{3,2},{4,5},{5,4},{6,7},{7,6},{8,9},{9,8},{10,11... | collective-permute-start | bytes 1572872 | tf_op jit(solution)/shard_map/ppermute | solution.py:269
  215.5 24.8 %collective-permute-start.43 = (bf16[4,264,512]{2,1,0:T(8,128)(2,1)S(1)}, bf16[4,264,512]{2,1,0:T(8,128)(2,1)S(1)}, u32[]{:S(2)}, u32[]{:S(2)}) collective-permute-start(bf16[4,264,512]{2,1,0:T(8,128)(2,1)S(1)} %get-tuple-element.223), channel_id=1, source_target_pairs={{0,2},{2,0},{1,3},{3,1},{4,6},{6,4},{5,7},{7,5},{8,10},{10,8},{9,1... | collective-permute-start | bytes 3244040 | tf_op jit(solution)/shard_map/ppermute | solution.py:269
  220.5 23.4 %collective-permute-start.44 = (bf16[256,512]{1,0:T(8,128)(2,1)S(1)}, bf16[256,512]{1,0:T(8,128)(2,1)S(1)}, u32[]{:S(2)}, u32[]{:S(2)}) collective-permute-start(bf16[256,512]{1,0:T(8,128)(2,1)S(1)} %get-tuple-element.218), channel_id=1, source_target_pairs={{0,12},{4,0},{8,4},{12,8},{1,13},{5,1},{9,5},{13,9},{2,14},{6,2},{... | collective-permute-start | bytes 786440 | tf_op jit(solution)/shard_map/ppermute | solution.py:274
  222.4 23.4 %collective-permute-start.45 = (bf16[256,512]{1,0:T(8,128)(2,1)S(1)}, bf16[256,512]{1,0:T(8,128)(2,1)S(1)}, u32[]{:S(2)}, u32[]{:S(2)}) collective-permute-start(bf16[256,512]{1,0:T(8,128)(2,1)S(1)} %get-tuple-element.219), channel_id=1, source_target_pairs={{0,8},{4,12},{8,0},{12,4},{1,9},{5,13},{9,1},{13,5},{2,10},{6,14},... | collective-permute-start | bytes 786440 | tf_op jit(solution)/shard_map/ppermute | solution.py:274
  222.4 24.1 %collective-permute-start.46 = (bf16[256,512]{1,0:T(8,128)(2,1)S(1)}, bf16[256,512]{1,0:T(8,128)(2,1)S(1)}, u32[]{:S(2)}, u32[]{:S(2)}) collective-permute-start(bf16[256,512]{1,0:T(8,128)(2,1)S(1)} %get-tuple-element.220), channel_id=1, source_target_pairs={{0,4},{4,8},{8,12},{12,0},{1,5},{5,9},{9,13},{13,1},{2,6},{6,10},{... | collective-permute-start | bytes 786440 | tf_op jit(solution)/shard_map/ppermute | solution.py:274
  222.8 24.4 %collective-permute-start.41 = (bf16[2,256,256]{2,1,0:T(8,128)(2,1)S(1)}, bf16[2,256,256]{2,1,0:T(8,128)(2,1)S(1)}, u32[]{:S(2)}, u32[]{:S(2)}) collective-permute-start(bf16[2,256,256]{2,1,0:T(8,128)(2,1)S(1)} %pad_maximum_fusion.11), channel_id=1, source_target_pairs={{0,16},{16,0},{1,17},{17,1},{2,18},{18,2},{3,19},{19,3},{4,20},{20... | collective-permute-start | bytes 786440 | tf_op jit(solution)/shard_map/ppermute | solution.py:269
  240.2 21.0 %collective-permute-start.50 = (bf16[2,2,272,256]{3,2,1,0:T(8,128)(2,1)}, bf16[2,2,272,256]{3,2,1,0:T(8,128)(2,1)}, u32[]{:S(2)}, u32[]{:S(2)}) collective-permute-start(bf16[2,2,272,256]{3,2,1,0:T(8,128)(2,1)} %get-tuple-element.229), channel_id=1, source_target_pairs={{0,2},{2,0},{1,3},{3,1},{4,6},{6,4},{5,7},{7,5},{8,10},{10,8},{9,1... | collective-permute-start | bytes 1671176 | tf_op jit(solution)/shard_map/ppermute | solution.py:269
  243.9 14.2 %collective-permute-start.47 = (bf16[264,512]{1,0:T(8,128)(2,1)S(1)}, bf16[264,512]{1,0:T(8,128)(2,1)S(1)}, u32[]{:S(2)}, u32[]{:S(2)}) collective-permute-start(bf16[264,512]{1,0:T(8,128)(2,1)S(1)} %get-tuple-element.231), channel_id=1, source_target_pairs={{0,12},{4,0},{8,4},{12,8},{1,13},{5,1},{9,5},{13,9},{2,14},{6,2},{... | collective-permute-start | bytes 811016 | tf_op jit(solution)/shard_map/ppermute | solution.py:274
  246.5 11.6 %collective-permute-start.48 = (bf16[264,512]{1,0:T(8,128)(2,1)S(1)}, bf16[264,512]{1,0:T(8,128)(2,1)S(1)}, u32[]{:S(2)}, u32[]{:S(2)}) collective-permute-start(bf16[264,512]{1,0:T(8,128)(2,1)S(1)} %get-tuple-element.233), channel_id=1, source_target_pairs={{0,4},{4,8},{8,12},{12,0},{1,5},{5,9},{9,13},{13,1},{2,6},{6,10},{... | collective-permute-start | bytes 811016 | tf_op jit(solution)/shard_map/ppermute | solution.py:274
  258.8 14.5 %collective-permute-start.49 = (bf16[2,2,272,256]{3,2,1,0:T(8,128)(2,1)}, bf16[2,2,272,256]{3,2,1,0:T(8,128)(2,1)}, u32[]{:S(2)}, u32[]{:S(2)}) collective-permute-start(bf16[2,2,272,256]{3,2,1,0:T(8,128)(2,1)} %get-tuple-element.237), channel_id=1, source_target_pairs={{0,2},{2,0},{1,3},{3,1},{4,6},{6,4},{5,7},{7,5},{8,10},{10,8},{9,1... | collective-permute-start | bytes 1671176 | tf_op jit(solution)/shard_map/ppermute | solution.py:269
  258.8 14.4 %collective-permute-start.51 = (bf16[264,512]{1,0:T(8,128)(2,1)}, bf16[264,512]{1,0:T(8,128)(2,1)}, u32[]{:S(2)}, u32[]{:S(2)}) collective-permute-start(bf16[264,512]{1,0:T(8,128)(2,1)} %get-tuple-element.232), channel_id=1, source_target_pairs={{0,8},{4,12},{8,0},{12,4},{1,9},{5,13},{9,1},{13,5},{2,10},{6,14},... | collective-permute-start | bytes 811016 | tf_op jit(solution)/shard_map/ppermute | solution.py:274
  275.9 7.7 %collective-permute-start.53 = (bf16[256,1024]{1,0:T(8,128)(2,1)S(1)}, bf16[256,1024]{1,0:T(8,128)(2,1)S(1)}, u32[]{:S(2)}, u32[]{:S(2)}) collective-permute-start(bf16[256,1024]{1,0:T(8,128)(2,1)S(1)} %fusion.16), channel_id=1, source_target_pairs={{0,16},{16,0},{1,17},{17,1},{2,18},{18,2},{3,19},{19,3},{4,20},{20... | collective-permute-start | bytes 1572872 | tf_op jit(solution)/shard_map/ppermute | solution.py:269
  278.1 15.4 %collective-permute-start.56 = (bf16[2,272,256]{2,1,0:T(8,128)(2,1)S(1)}, bf16[2,272,256]{2,1,0:T(8,128)(2,1)S(1)}, u32[]{:S(2)}, u32[]{:S(2)}) collective-permute-start(bf16[2,272,256]{2,1,0:T(8,128)(2,1)S(1)} %get-tuple-element.240), channel_id=1, source_target_pairs={{0,12},{4,0},{8,4},{12,8},{1,13},{5,1},{9,5},{13,9},{2,14},{6,2},{... | collective-permute-start | bytes 835592 | tf_op jit(solution)/shard_map/ppermute | solution.py:274
  280.8 10.8 %collective-permute-start.52 = (bf16[256,1024]{1,0:T(8,128)(2,1)S(1)}, bf16[256,1024]{1,0:T(8,128)(2,1)S(1)}, u32[]{:S(2)}, u32[]{:S(2)}) collective-permute-start(bf16[256,1024]{1,0:T(8,128)(2,1)S(1)} %pad_maximum_fusion.6), channel_id=1, source_target_pairs={{0,0},{2,16},{16,2},{18,18},{1,1},{3,17},{17,3},{19,19},{4,4},{6,2... | collective-permute-start | bytes 1572872 | tf_op jit(solution)/shard_map/ppermute | solution.py:1053
  284.0 24.2 %collective-permute-start.55 = (bf16[256,1024]{1,0:T(8,128)(2,1)S(1)}, bf16[256,1024]{1,0:T(8,128)(2,1)S(1)}, u32[]{:S(2)}, u32[]{:S(2)}) collective-permute-start(bf16[256,1024]{1,0:T(8,128)(2,1)S(1)} %fusion.15), channel_id=1, source_target_pairs={{0,1},{1,0},{2,3},{3,2},{4,5},{5,4},{6,7},{7,6},{8,9},{9,8},{10,11... | collective-permute-start | bytes 1572872 | tf_op jit(solution)/shard_map/ppermute | solution.py:269
  287.4 20.9 %collective-permute-start.54 = (bf16[256,1024]{1,0:T(8,128)(2,1)S(1)}, bf16[256,1024]{1,0:T(8,128)(2,1)S(1)}, u32[]{:S(2)}, u32[]{:S(2)}) collective-permute-start(bf16[256,1024]{1,0:T(8,128)(2,1)S(1)} %get-tuple-element.257), channel_id=1, source_target_pairs={{0,16},{16,0},{1,17},{17,1},{2,18},{18,2},{3,19},{19,3},{4,20},{20... | collective-permute-start | bytes 1572872 | tf_op jit(solution)/shard_map/ppermute | solution.py:269
  287.4 20.8 %collective-permute-start.57 = (bf16[2,272,256]{2,1,0:T(8,128)(2,1)S(1)}, bf16[2,272,256]{2,1,0:T(8,128)(2,1)S(1)}, u32[]{:S(2)}, u32[]{:S(2)}) collective-permute-start(bf16[2,272,256]{2,1,0:T(8,128)(2,1)S(1)} %get-tuple-element.241), channel_id=1, source_target_pairs={{0,8},{4,12},{8,0},{12,4},{1,9},{5,13},{9,1},{13,5},{2,10},{6,14},... | collective-permute-start | bytes 835592 | tf_op jit(solution)/shard_map/ppermute | solution.py:274
  291.6 16.7 %collective-permute-start.58 = (bf16[2,272,256]{2,1,0:T(8,128)(2,1)S(1)}, bf16[2,272,256]{2,1,0:T(8,128)(2,1)S(1)}, u32[]{:S(2)}, u32[]{:S(2)}) collective-permute-start(bf16[2,272,256]{2,1,0:T(8,128)(2,1)S(1)} %get-tuple-element.242), channel_id=1, source_target_pairs={{0,4},{4,8},{8,12},{12,0},{1,5},{5,9},{9,13},{13,1},{2,6},{6,10},{... | collective-permute-start | bytes 835592 | tf_op jit(solution)/shard_map/ppermute | solution.py:274
  293.4 14.8 %collective-permute-start.59 = (bf16[520,256]{1,0:T(8,128)(2,1)S(1)}, bf16[520,256]{1,0:T(8,128)(2,1)S(1)}, u32[]{:S(2)}, u32[]{:S(2)}) collective-permute-start(bf16[520,256]{1,0:T(8,128)(2,1)S(1)} %get-tuple-element.261), channel_id=1, source_target_pairs={{0,1},{1,0},{2,3},{3,2},{4,5},{5,4},{6,7},{7,6},{8,9},{9,8},{10,11... | collective-permute-start | bytes 798728 | tf_op jit(solution)/shard_map/ppermute | solution.py:269
  309.6 10.5 %collective-permute-start.60 = (bf16[256,1024]{1,0:T(8,128)(2,1)S(1)}, bf16[256,1024]{1,0:T(8,128)(2,1)S(1)}, u32[]{:S(2)}, u32[]{:S(2)}) collective-permute-start(bf16[256,1024]{1,0:T(8,128)(2,1)S(1)} %add_convert_fusion), channel_id=1, source_target_pairs={{0,0},{2,16},{16,2},{18,18},{1,1},{3,17},{17,3},{19,19},{4,4},{6,2... | collective-permute-start | bytes 1572872 | tf_op jit(solution)/shard_map/ppermute | solution.py:1067
  (86 other events, 945.4 us)

commit v2 on v1

--- a/solution.py
+++ b/solution.py
@@ -262,7 +262,7 @@
 PAIR = ((0, 1), (1, 0))
 MEBIBYTE = 1024 * 1024
 BLOCK = 256
-QUERIES = 512
+QUERIES = 1024
 
 
 def flip(values, axis_name):

time: 332 us -> 332 us (level)
  no operation moved by 1% of the time
where the time goes in v2:
time: 332 us; the launch traced here: 327 us
  waiting for transfers between devices  157 us (47%)
  Pallas kernels  69 us (21%)
  starting transfers between devices  68.8 us (21%)
  matrix products  15 us (5%)
  local copies, waits for them, and re-layouts  7.99 us (2%)
  other arithmetic  7.09 us (2%)
    ppermute x42, waiting for transfers between devices, flip(): return lax.ppermute(values, axis_name, PAIR)  84.1 us
    pallas_call x23, Pallas kernels, kernel_call(): pl.pallas_call(kernel, grid_spec=pltpu.PrefetchScalarGridSpec(num_scalar_...  69 us
    ppermute x18, waiting for transfers between devices, shift(): lax.ppermute(values, axis_name, [(i, (i + step) % size) for i in range(si...  64 us
    ppermute x42, starting transfers between devices, flip(): return lax.ppermute(values, axis_name, PAIR)  38.6 us
    ppermute x18, starting transfers between devices, shift(): lax.ppermute(values, axis_name, [(i, (i + step) % size) for i in range(si...  17.1 us
  transfers between devices with their start and end apart: 64, of which 27 were waited for; matrix products, arithmetic and copies ran while one was open for 4% of the time, Pallas kernels for 19%

profile of v2, /device:TPU:1, one launch (start us, length us, event | category | flops | bytes accessed | tf_op | source)
XLA Modules:
  0.0 327.0 jit_solution(4696138615147132360)
XLA Ops:
  0.7 4.7 %collective-permute-start = (bf16[256,1024]{1,0:T(8,128)(2,1)}, bf16[256,1024]{1,0:T(8,128)(2,1)S(1)}, u32[]{:S(2)}, u32[]{:S(2)}) collective-permute-start(bf16[256,1024]{1,0:T(8,128)(2,1)} %param.14), channel_id=1, source_target_pairs={{0,0},{2,16},{16,2},{18,18},{1,1},{3,17},{17,3},{19,19},{4,4},{6,2... | collective-permute-start | bytes 1572872 | tf_op jit(solution)/shard_map/ppermute | solution.py:700
  6.0 2.7 prepare_attn.1
  9.9 2.7 prepare_ff.1
  15.2 2.7 collective-permute-start.13
  18.0 3.4 %collective-permute-start.7 = (bf16[2,200,256]{2,1,0:T(8,128)(2,1)S(1)}, bf16[2,200,256]{2,1,0:T(8,128)(2,1)S(1)}, u32[]{:S(2)}, u32[]{:S(2)}) collective-permute-start(bf16[2,200,256]{2,1,0:T(8,128)(2,1)S(1)} %get-tuple-element.307), channel_id=1, source_target_pairs={{0,12},{4,0},{8,4},{12,8},{1,13},{5,1},{9,5},{13,9},{2,14},{6,2},{... | collective-permute-start | bytes 614408 | tf_op jit(solution)/shard_map/ppermute | solution.py:274
  23.4 2.9 collective-permute-done.7
  26.3 10.8 %collective-permute-done.6 = bf16[2,200,256]{2,1,0:T(8,128)(2,1)S(1)} collective-permute-done((bf16[2,200,256]{2,1,0:T(8,128)(2,1)S(1)}, bf16[2,200,256]{2,1,0:T(8,128)(2,1)S(1)}, u32[]{:S(2)}, u32[]{:S(2)}) %collective-permute-start.6) | collective-permute-done | bytes 204832 | tf_op jit(solution)/shard_map/ppermute | solution.py:274
  40.0 5.4 %collective-permute-done.14 = bf16[2,256,256]{2,1,0:T(8,128)(2,1)S(1)} collective-permute-done((bf16[2,256,256]{2,1,0:T(8,128)(2,1)S(1)}, bf16[2,256,256]{2,1,0:T(8,128)(2,1)S(1)}, u32[]{:S(2)}, u32[]{:S(2)}) %collective-permute-start.14) | collective-permute-done | bytes 262176 | tf_op jit(solution)/shard_map/ppermute | solution.py:269
  45.4 2.6 collective-permute-start.11
  49.4 8.1 %collective-permute-done.8.far = bf16[4,2,200,256]{3,2,1,0:T(8,128)(2,1)S(1)} collective-permute-done((bf16[4,2,200,256]{3,2,1,0:T(8,128)(2,1)S(1)}, bf16[4,2,200,256]{3,2,1,0:T(8,128)(2,1)S(1)}, u32[]{:S(2)}, u32[]{:S(2)}) %collective-permute-start.8) | collective-permute-done | bytes 819232 | tf_op jit(solution)/shard_map/ppermute | solution.py:269
  57.5 5.1 %attend.2 = (bf16[2,3,64,1024]{3,2,1,0:T(8,128)(2,1)S(1)}, f32[2,64,1024]{2,1,0:T(8,128)S(1)}, f32[2,1,1024]{2,1,0:T(1,128)S(1)}, bf16[2,192,256]{2,1,0:T(8,128)...) custom-call(s32[6]{0:T(128)S(1)} %copy-done.44, ...), custom_call_target="tpu_custom_call" | custom-call | flops 10000000000 | bytes 100000000 | tf_op jit(solution)/shard_map/attend/pallas_call | solution.py:302
  62.6 9.6 %collective-permute-done.11 = bf16[336,512]{1,0:T(8,128)(2,1)S(1)} collective-permute-done((bf16[336,512]{1,0:T(8,128)(2,1)S(1)}, bf16[336,512]{1,0:T(8,128)(2,1)S(1)}, u32[]{:S(2)}, u32[]{:S(2)}) %collective-permute-start.11) | collective-permute-done | bytes 344096 | tf_op jit(solution)/shard_map/ppermute | solution.py:274
  75.9 5.0 %attend.3 = (bf16[2,3,64,1024]{3,2,1,0:T(8,128)(2,1)S(1)}, f32[2,64,1024]{2,1,0:T(8,128)S(1)}, f32[2,1,1024]{2,1,0:T(1,128)S(1)}, bf16[2,192,256]{2,1,0:T(8,128)...) custom-call(s32[6]{0:T(128)S(1)} %copy-done.44, ...), custom_call_target="tpu_custom_call" | custom-call | flops 10000000000 | bytes 100000000 | tf_op jit(solution)/shard_map/attend/pallas_call | solution.py:302
  81.1 5.0 %collective-permute-done.16 = bf16[256,512]{1,0:T(8,128)(2,1)S(1)} collective-permute-done((bf16[256,512]{1,0:T(8,128)(2,1)S(1)}, bf16[256,512]{1,0:T(8,128)(2,1)S(1)}, u32[]{:S(2)}, u32[]{:S(2)}) %collective-permute-start.16) | collective-permute-done | bytes 262176 | tf_op jit(solution)/shard_map/ppermute | solution.py:274
  92.2 10.3 %collective-permute-done.21 = bf16[256,512]{1,0:T(8,128)(2,1)S(1)} collective-permute-done((bf16[256,512]{1,0:T(8,128)(2,1)S(1)}, bf16[256,512]{1,0:T(8,128)(2,1)S(1)}, u32[]{:S(2)}, u32[]{:S(2)}) %collective-permute-start.21) | collective-permute-done | bytes 262176 | tf_op jit(solution)/shard_map/ppermute | solution.py:274
  102.5 2.3 collective-permute-done.20
  104.8 1.7 out_near.1
  106.6 2.2 collective-permute-start.22
  112.4 2.5 norm1.1
  118.3 10.2 %collective-permute-done.25.r2 = bf16[256,1024]{1,0:T(8,128)(2,1)S(1)} collective-permute-done((bf16[256,1024]{1,0:T(8,128)(2,1)S(1)}, bf16[256,1024]{1,0:T(8,128)(2,1)S(1)}, u32[]{:S(2)}, u32[]{:S(2)}) %collective-permute-start.25) | collective-permute-done | bytes 524320 | tf_op jit(solution)/shard_map/ppermute | solution.py:269
  129.6 6.1 %collective-permute-done.27 = bf16[4,256,512]{2,1,0:T(8,128)(2,1)S(1)} collective-permute-done((bf16[4,256,512]{2,1,0:T(8,128)(2,1)S(1)}, bf16[4,256,512]{2,1,0:T(8,128)(2,1)S(1)}, u32[]{:S(2)}, u32[]{:S(2)}) %collective-permute-start.27) | collective-permute-done | bytes 1048608 | tf_op jit(solution)/shard_map/ppermute | solution.py:269
  145.5 10.3 %collective-permute-done.30.got = bf16[256,1024]{1,0:T(8,128)(2,1)S(1)} collective-permute-done((bf16[256,1024]{1,0:T(8,128)(2,1)S(1)}, bf16[256,1024]{1,0:T(8,128)(2,1)S(1)}, u32[]{:S(2)}, u32[]{:S(2)}) %collective-permute-start.30) | collective-permute-done | bytes 524320 | tf_op jit(solution)/shard_map/ppermute | solution.py:269
  155.8 2.8 norm2.1
  161.2 1.8 fusion.5.left_near
  162.9 10.2 %collective-permute-done.32.r2 = bf16[256,1024]{1,0:T(8,128)(2,1)S(1)} collective-permute-done((bf16[256,1024]{1,0:T(8,128)(2,1)S(1)}, bf16[256,1024]{1,0:T(8,128)(2,1)S(1)}, u32[]{:S(2)}, u32[]{:S(2)}) %collective-permute-start.32) | collective-permute-done | bytes 524320 | tf_op jit(solution)/shard_map/ppermute | solution.py:269
  175.5 1.8 fusion.11.left_far
  184.0 4.0 %weight_grad.3 = (bf16[4,256,512]{2,1,0:T(8,128)(2,1)S(1)}, bf16[4,256,512]{2,1,0:T(8,128)(2,1)S(1)}) custom-call(s32[6]{0:T(128)S(1)} %copy-done.44, bf16[512,1024]{1,0:T(8,128)(2,1)S(1)} %get-tuple-element.207.left_near, bf16[512,1024]{1,0:T(8,128)(2,1)S(1)} %get-tuple-element.208.left_far, bf16[256,1024]{1,0:T(8,128)(2,1)S(1)} %get-tuple-element.195.r0, ...), custom_call_target="tpu_custom_call" | custom-call | flops 10000000000 | bytes 100000000 | tf_op jit(solution)/shard_map/weight_grad/pallas_call | solution.py:302
  189.6 4.0 %weight_grad.2 = (bf16[4,264,512]{2,1,0:T(8,128)(2,1)S(1)}, bf16[4,264,512]{2,1,0:T(8,128)(2,1)S(1)}) custom-call(s32[6]{0:T(128)S(1)} %copy-done.44, bf16[512,1024]{1,0:T(8,128)(2,1)S(1)} %fusion.5.left_near, bf16[512,1024]{1,0:T(8,128)(2,1)S(1)} %fusion.11.left_far, bf16[256,1024]{1,0:T(8,128)(2,1)S(1)} %get-tuple-element.180.r0, ...), custom_call_target="tpu_custom_call" | custom-call | flops 10000000000 | bytes 100000000 | tf_op jit(solution)/shard_map/weight_grad/pallas_call | solution.py:302
  193.6 1.8 collective-permute-done.36.got
  198.2 14.7 %collective-permute-done.38.got = bf16[4,256,512]{2,1,0:T(8,128)(2,1)S(1)} collective-permute-done((bf16[4,256,512]{2,1,0:T(8,128)(2,1)S(1)}, bf16[4,256,512]{2,1,0:T(8,128)(2,1)S(1)}, u32[]{:S(2)}, u32[]{:S(2)}) %collective-permute-start.38) | collective-permute-done | bytes 1048608 | tf_op jit(solution)/shard_map/ppermute | solution.py:269
  217.0 1.9 out_back.1
  220.5 1.9 collective-permute-start.44
  224.4 10.3 %attend_back.2 = (bf16[2,192,1024]{2,1,0:T(8,128)(2,1)S(1)}, bf16[2,2,272,256]{3,2,1,0:T(8,128)(2,1)S(1)}, bf16[2,2,272,256]{3,2,1,0:T(8,128)(2,1)}) custom-call(s32[6]{0:T(128)S(1)} %copy-done.44, bf16[2,3,64,1024]{3,2,1,0:T(8,128)(2,1)S(1)} %copy-done.48, bf16[4,64,1024]{2,1,0:T(8,128)(2,1)S(1)} %get-tuple-element.234.grad_ref, ...), custom_call_target="tpu_custom_call" | custom-call | flops 10000000000 | bytes 100000000 | tf_op jit(solution)/shard_map/attend_back/pallas_call | solution.py:302
  234.7 5.5 %collective-permute-done.43.got = bf16[4,264,512]{2,1,0:T(8,128)(2,1)S(1)} collective-permute-done((bf16[4,264,512]{2,1,0:T(8,128)(2,1)S(1)}, bf16[4,264,512]{2,1,0:T(8,128)(2,1)S(1)}, u32[]{:S(2)}, u32[]{:S(2)}) %collective-permute-start.43) | collective-permute-done | bytes 1081376 | tf_op jit(solution)/shard_map/ppermute | solution.py:269
  243.9 1.9 collective-permute-start.47
  247.2 10.0 %attend_back.3 = (bf16[2,192,1024]{2,1,0:T(8,128)(2,1)S(1)}, bf16[2,2,272,256]{3,2,1,0:T(8,128)(2,1)S(1)}, bf16[2,2,272,256]{3,2,1,0:T(8,128)(2,1)}) custom-call(s32[6]{0:T(128)S(1)} %copy-done.44, bf16[2,3,64,1024]{3,2,1,0:T(8,128)(2,1)S(1)} %copy-done.46, bf16[4,64,1024]{2,1,0:T(8,128)(2,1)S(1)} %get-tuple-element.234.grad_ref, ...), custom_call_target="tpu_custom_call" | custom-call | flops 10000000000 | bytes 100000000 | tf_op jit(solution)/shard_map/attend_back/pallas_call | solution.py:302
  261.3 12.0 %collective-permute-done.51.refs_6_ = bf16[264,512]{1,0:T(8,128)(2,1)} collective-permute-done((bf16[264,512]{1,0:T(8,128)(2,1)}, bf16[264,512]{1,0:T(8,128)(2,1)}, u32[]{:S(2)}, u32[]{:S(2)}) %collective-permute-start.51) | collective-permute-done | bytes 270368 | tf_op jit(solution)/shard_map/ppermute | solution.py:274
  273.2 2.1 tail_sum.1
  278.1 2.7 collective-permute-start.56
  280.8 2.7 collective-permute-start.52
  285.4 2.0 input_near.1
  287.5 4.1 %collective-permute-done.52 = bf16[256,1024]{1,0:T(8,128)(2,1)S(1)} collective-permute-done((bf16[256,1024]{1,0:T(8,128)(2,1)S(1)}, bf16[256,1024]{1,0:T(8,128)(2,1)S(1)}, u32[]{:S(2)}, u32[]{:S(2)}) %collective-permute-start.52) | collective-permute-done | bytes 524320 | tf_op jit(solution)/shard_map/ppermute | solution.py:1053
  291.6 1.8 last_ff.1
  294.7 13.5 %collective-permute-done.57.refs_1_ = bf16[2,272,256]{2,1,0:T(8,128)(2,1)S(1)} collective-permute-done((bf16[2,272,256]{2,1,0:T(8,128)(2,1)S(1)}, bf16[2,272,256]{2,1,0:T(8,128)(2,1)S(1)}, u32[]{:S(2)}, u32[]{:S(2)}) %collective-permute-start.57) | collective-permute-done | bytes 278560 | tf_op jit(solution)/shard_map/ppermute | solution.py:274
  309.6 3.0 collective-permute-start.60
  315.5 4.5 %collective-permute-done.60 = bf16[256,1024]{1,0:T(8,128)(2,1)S(1)} collective-permute-done((bf16[256,1024]{1,0:T(8,128)(2,1)S(1)}, bf16[256,1024]{1,0:T(8,128)(2,1)S(1)}, u32[]{:S(2)}, u32[]{:S(2)}) %collective-permute-start.60) | collective-permute-done | bytes 524320 | tf_op jit(solution)/shard_map/ppermute | solution.py:1067
  321.3 2.1 last_ff_out.1
  323.4 1.8 last.1
  (298 shorter events, 83.7 us)
Async XLA Ops:
  0.7 13.1 %collective-permute-start = (bf16[256,1024]{1,0:T(8,128)(2,1)}, bf16[256,1024]{1,0:T(8,128)(2,1)S(1)}, u32[]{:S(2)}, u32[]{:S(2)}) collective-permute-start(bf16[256,1024]{1,0:T(8,128)(2,1)} %param.14), channel_id=1, source_target_pairs={{0,0},{2,16},{16,2},{18,18},{1,1},{3,17},{17,3},{19,19},{4,4},{6,2... | collective-permute-start | bytes 1572872 | tf_op jit(solution)/shard_map/ppermute | solution.py:700
  12.6 8.7 %collective-permute-start.9 = (bf16[512,256]{1,0:T(8,128)(2,1)}, bf16[512,256]{1,0:T(8,128)(2,1)S(1)}, u32[]{:S(2)}, u32[]{:S(2)}) collective-permute-start(bf16[512,256]{1,0:T(8,128)(2,1)} %get-tuple-element.154), channel_id=1, source_target_pairs={{0,1},{1,0},{2,3},{3,2},{4,5},{5,4},{6,7},{7,6},{8,9},{9,8},{10,11... | collective-permute-start | bytes 786440 | tf_op jit(solution)/shard_map/ppermute | solution.py:269
  13.8 23.3 %collective-permute-start.2 = (bf16[256,1024]{1,0:T(8,128)(2,1)S(1)}, bf16[256,1024]{1,0:T(8,128)(2,1)S(1)}, u32[]{:S(2)}, u32[]{:S(2)}) collective-permute-start(bf16[256,1024]{1,0:T(8,128)(2,1)S(1)} %collective-permute-done.x00.refs_0_), channel_id=1, source_target_pairs={{0,1},{1,0},{2,3},{3,2},{4,5},{5,4},{6,7},{7,6},{8,9},{9,8},{10,11... | collective-permute-start | bytes 1572872 | tf_op jit(solution)/shard_map/ppermute | solution.py:269
  15.2 22.0 %collective-permute-start.13 = (bf16[256,1024]{1,0:T(8,128)(2,1)S(1)}, bf16[256,1024]{1,0:T(8,128)(2,1)S(1)}, u32[]{:S(2)}, u32[]{:S(2)}) collective-permute-start(bf16[256,1024]{1,0:T(8,128)(2,1)S(1)} %copy-done.69), channel_id=1, source_target_pairs={{0,0},{2,16},{16,2},{18,18},{1,1},{3,17},{17,3},{19,19},{4,4},{6,2... | collective-permute-start | bytes 1572872 | tf_op jit(solution)/shard_map/ppermute | solution.py:728
  18.0 8.3 %collective-permute-start.7 = (bf16[2,200,256]{2,1,0:T(8,128)(2,1)S(1)}, bf16[2,200,256]{2,1,0:T(8,128)(2,1)S(1)}, u32[]{:S(2)}, u32[]{:S(2)}) collective-permute-start(bf16[2,200,256]{2,1,0:T(8,128)(2,1)S(1)} %get-tuple-element.307), channel_id=1, source_target_pairs={{0,12},{4,0},{8,4},{12,8},{1,13},{5,1},{9,5},{13,9},{2,14},{6,2},{... | collective-permute-start | bytes 614408 | tf_op jit(solution)/shard_map/ppermute | solution.py:274
  21.3 15.7 %collective-permute-start.6 = (bf16[2,200,256]{2,1,0:T(8,128)(2,1)S(1)}, bf16[2,200,256]{2,1,0:T(8,128)(2,1)S(1)}, u32[]{:S(2)}, u32[]{:S(2)}) collective-permute-start(bf16[2,200,256]{2,1,0:T(8,128)(2,1)S(1)} %get-tuple-element.307), channel_id=1, source_target_pairs={{0,8},{4,12},{8,0},{12,4},{1,9},{5,13},{9,1},{13,5},{2,10},{6,14},... | collective-permute-start | bytes 614408 | tf_op jit(solution)/shard_map/ppermute | solution.py:274
  21.3 15.7 %collective-permute-start.5 = (bf16[2,200,256]{2,1,0:T(8,128)(2,1)S(1)}, bf16[2,200,256]{2,1,0:T(8,128)(2,1)S(1)}, u32[]{:S(2)}, u32[]{:S(2)}) collective-permute-start(bf16[2,200,256]{2,1,0:T(8,128)(2,1)S(1)} %get-tuple-element.307), channel_id=1, source_target_pairs={{0,4},{4,8},{8,12},{12,0},{1,5},{5,9},{9,13},{13,1},{2,6},{6,10},{... | collective-permute-start | bytes 614408 | tf_op jit(solution)/shard_map/ppermute | solution.py:274
  37.3 8.1 %collective-permute-start.14 = (bf16[2,256,256]{2,1,0:T(8,128)(2,1)S(1)}, bf16[2,256,256]{2,1,0:T(8,128)(2,1)S(1)}, u32[]{:S(2)}, u32[]{:S(2)}) collective-permute-start(bf16[2,256,256]{2,1,0:T(8,128)(2,1)S(1)} %pad_maximum_fusion.9), channel_id=1, source_target_pairs={{0,1},{1,0},{2,3},{3,2},{4,5},{5,4},{6,7},{7,6},{8,9},{9,8},{10,11... | collective-permute-start | bytes 786440 | tf_op jit(solution)/shard_map/ppermute | solution.py:269
  37.7 19.8 %collective-permute-start.8 = (bf16[4,2,200,256]{3,2,1,0:T(8,128)(2,1)S(1)}, bf16[4,2,200,256]{3,2,1,0:T(8,128)(2,1)S(1)}, u32[]{:S(2)}, u32[]{:S(2)}) collective-permute-start(bf16[4,2,200,256]{3,2,1,0:T(8,128)(2,1)S(1)} %pad_maximum_fusion.4.own), channel_id=1, source_target_pairs={{0,2},{2,0},{1,3},{3,1},{4,6},{6,4},{5,7},{7,5},{8,10},{10,8},{9,1... | collective-permute-start | bytes 2457608 | tf_op jit(solution)/shard_map/ppermute | solution.py:269
  38.4 9.7 %collective-permute-start.3 = (bf16[256,1024]{1,0:T(8,128)(2,1)S(1)}, bf16[256,1024]{1,0:T(8,128)(2,1)S(1)}, u32[]{:S(2)}, u32[]{:S(2)}) collective-permute-start(bf16[256,1024]{1,0:T(8,128)(2,1)S(1)} %collective-permute-done.x00.refs_0_), channel_id=1, source_target_pairs={{0,16},{16,0},{1,17},{17,1},{2,18},{18,2},{3,19},{19,3},{4,20},{20... | collective-permute-start | bytes 1572872 | tf_op jit(solution)/shard_map/ppermute | solution.py:269
  39.8 8.4 %collective-permute-start.4 = (bf16[256,1024]{1,0:T(8,128)(2,1)S(1)}, bf16[256,1024]{1,0:T(8,128)(2,1)S(1)}, u32[]{:S(2)}, u32[]{:S(2)}) collective-permute-start(bf16[256,1024]{1,0:T(8,128)(2,1)S(1)} %collective-permute-done.2.x01.refs_1_), channel_id=1, source_target_pairs={{0,16},{16,0},{1,17},{17,1},{2,18},{18,2},{3,19},{19,3},{4,20},{20... | collective-permute-start | bytes 1572872 | tf_op jit(solution)/shard_map/ppermute | solution.py:269
  39.9 22.6 %collective-permute-start.12 = (bf16[336,512]{1,0:T(8,128)(2,1)S(1)}, bf16[336,512]{1,0:T(8,128)(2,1)S(1)}, u32[]{:S(2)}, u32[]{:S(2)}) collective-permute-start(bf16[336,512]{1,0:T(8,128)(2,1)S(1)} %fusion.46), channel_id=1, source_target_pairs={{0,12},{4,0},{8,4},{12,8},{1,13},{5,1},{9,5},{13,9},{2,14},{6,2},{... | collective-permute-start | bytes 1032200 | tf_op jit(solution)/shard_map/ppermute | solution.py:274
  45.4 26.7 %collective-permute-start.11 = (bf16[336,512]{1,0:T(8,128)(2,1)S(1)}, bf16[336,512]{1,0:T(8,128)(2,1)S(1)}, u32[]{:S(2)}, u32[]{:S(2)}) collective-permute-start(bf16[336,512]{1,0:T(8,128)(2,1)S(1)} %fusion.46), channel_id=1, source_target_pairs={{0,8},{4,12},{8,0},{12,4},{1,9},{5,13},{9,1},{13,5},{2,10},{6,14},... | collective-permute-start | bytes 1032200 | tf_op jit(solution)/shard_map/ppermute | solution.py:274
  48.1 24.0 %collective-permute-start.10 = (bf16[336,512]{1,0:T(8,128)(2,1)S(1)}, bf16[336,512]{1,0:T(8,128)(2,1)S(1)}, u32[]{:S(2)}, u32[]{:S(2)}) collective-permute-start(bf16[336,512]{1,0:T(8,128)(2,1)S(1)} %fusion.46), channel_id=1, source_target_pairs={{0,4},{4,8},{8,12},{12,0},{1,5},{5,9},{9,13},{13,1},{2,6},{6,10},{... | collective-permute-start | bytes 1032200 | tf_op jit(solution)/shard_map/ppermute | solution.py:274
  48.2 24.0 %collective-permute-start.15 = (bf16[2,256,256]{2,1,0:T(8,128)(2,1)S(1)}, bf16[2,256,256]{2,1,0:T(8,128)(2,1)S(1)}, u32[]{:S(2)}, u32[]{:S(2)}) collective-permute-start(bf16[2,256,256]{2,1,0:T(8,128)(2,1)S(1)} %pad_maximum_fusion.10), channel_id=1, source_target_pairs={{0,16},{16,0},{1,17},{17,1},{2,18},{18,2},{3,19},{19,3},{4,20},{20... | collective-permute-start | bytes 786440 | tf_op jit(solution)/shard_map/ppermute | solution.py:269
  72.4 8.7 %collective-permute-start.17 = (bf16[256,512]{1,0:T(8,128)(2,1)S(1)}, bf16[256,512]{1,0:T(8,128)(2,1)S(1)}, u32[]{:S(2)}, u32[]{:S(2)}) collective-permute-start(bf16[256,512]{1,0:T(8,128)(2,1)S(1)} %get-tuple-element.175), channel_id=1, source_target_pairs={{0,12},{4,0},{8,4},{12,8},{1,13},{5,1},{9,5},{13,9},{2,14},{6,2},{... | collective-permute-start | bytes 786440 | tf_op jit(solution)/shard_map/ppermute | solution.py:274
  72.4 13.6 %collective-permute-start.16 = (bf16[256,512]{1,0:T(8,128)(2,1)S(1)}, bf16[256,512]{1,0:T(8,128)(2,1)S(1)}, u32[]{:S(2)}, u32[]{:S(2)}) collective-permute-start(bf16[256,512]{1,0:T(8,128)(2,1)S(1)} %get-tuple-element.175), channel_id=1, source_target_pairs={{0,4},{4,8},{8,12},{12,0},{1,5},{5,9},{9,13},{13,1},{2,6},{6,10},{... | collective-permute-start | bytes 786440 | tf_op jit(solution)/shard_map/ppermute | solution.py:274
  74.2 11.8 %collective-permute-start.18 = (bf16[4,72,512]{2,1,0:T(8,128)(2,1)S(1)}, bf16[4,72,512]{2,1,0:T(8,128)(2,1)S(1)}, u32[]{:S(2)}, u32[]{:S(2)}) collective-permute-start(bf16[4,72,512]{2,1,0:T(8,128)(2,1)S(1)} %slice.171.own), channel_id=1, source_target_pairs={{0,2},{2,0},{1,3},{3,1},{4,6},{6,4},{5,7},{7,5},{8,10},{10,8},{9,1... | collective-permute-start | bytes 884744 | tf_op jit(solution)/shard_map/ppermute | solution.py:269
  75.8 29.0 %collective-permute-start.20 = (bf16[4,264,512]{2,1,0:T(8,128)(2,1)S(1)}, bf16[4,264,512]{2,1,0:T(8,128)(2,1)S(1)}, u32[]{:S(2)}, u32[]{:S(2)}) collective-permute-start(bf16[4,264,512]{2,1,0:T(8,128)(2,1)S(1)} %slice.172), channel_id=1, source_target_pairs={{0,2},{2,0},{1,3},{3,1},{4,6},{6,4},{5,7},{7,5},{8,10},{10,8},{9,1... | collective-permute-start | bytes 3244040 | tf_op jit(solution)/shard_map/ppermute | solution.py:269
  88.5 14.0 %collective-permute-start.21 = (bf16[256,512]{1,0:T(8,128)(2,1)S(1)}, bf16[256,512]{1,0:T(8,128)(2,1)S(1)}, u32[]{:S(2)}, u32[]{:S(2)}) collective-permute-start(bf16[256,512]{1,0:T(8,128)(2,1)S(1)} %get-tuple-element.175), channel_id=1, source_target_pairs={{0,8},{4,12},{8,0},{12,4},{1,9},{5,13},{9,1},{13,5},{2,10},{6,14},... | collective-permute-start | bytes 786440 | tf_op jit(solution)/shard_map/ppermute | solution.py:274
  91.0 21.4 %collective-permute-start.23 = (bf16[256,1024]{1,0:T(8,128)(2,1)}, bf16[256,1024]{1,0:T(8,128)(2,1)}, u32[]{:S(2)}, u32[]{:S(2)}) collective-permute-start(bf16[256,1024]{1,0:T(8,128)(2,1)} %add_convert_fusion.2), channel_id=1, source_target_pairs={{0,1},{1,0},{2,3},{3,2},{4,5},{5,4},{6,7},{7,6},{8,9},{9,8},{10,11... | collective-permute-start | bytes 1572872 | tf_op jit(solution)/shard_map/ppermute | solution.py:269
  110.9 24.8 %collective-permute-start.27 = (bf16[4,256,512]{2,1,0:T(8,128)(2,1)S(1)}, bf16[4,256,512]{2,1,0:T(8,128)(2,1)S(1)}, u32[]{:S(2)}, u32[]{:S(2)}) collective-permute-start(bf16[4,256,512]{2,1,0:T(8,128)(2,1)S(1)} %pad_maximum_fusion.3), channel_id=1, source_target_pairs={{0,2},{2,0},{1,3},{3,1},{4,6},{6,4},{5,7},{7,5},{8,10},{10,8},{9,1... | collective-permute-start | bytes 3145736 | tf_op jit(solution)/shard_map/ppermute | solution.py:269
  115.3 13.3 %collective-permute-start.25 = (bf16[256,1024]{1,0:T(8,128)(2,1)S(1)}, bf16[256,1024]{1,0:T(8,128)(2,1)S(1)}, u32[]{:S(2)}, u32[]{:S(2)}) collective-permute-start(bf16[256,1024]{1,0:T(8,128)(2,1)S(1)} %get-tuple-element.180.r0), channel_id=1, source_target_pairs={{0,1},{1,0},{2,3},{3,2},{4,5},{5,4},{6,7},{7,6},{8,9},{9,8},{10,11... | collective-permute-start | bytes 1572872 | tf_op jit(solution)/shard_map/ppermute | solution.py:269
  142.5 13.4 %collective-permute-start.30 = (bf16[256,1024]{1,0:T(8,128)(2,1)S(1)}, bf16[256,1024]{1,0:T(8,128)(2,1)S(1)}, u32[]{:S(2)}, u32[]{:S(2)}) collective-permute-start(bf16[256,1024]{1,0:T(8,128)(2,1)S(1)} %fusion.17), channel_id=1, source_target_pairs={{0,1},{1,0},{2,3},{3,2},{4,5},{5,4},{6,7},{7,6},{8,9},{9,8},{10,11... | collective-permute-start | bytes 1572872 | tf_op jit(solution)/shard_map/ppermute | solution.py:269
  159.6 13.5 %collective-permute-start.32 = (bf16[256,1024]{1,0:T(8,128)(2,1)S(1)}, bf16[256,1024]{1,0:T(8,128)(2,1)S(1)}, u32[]{:S(2)}, u32[]{:S(2)}) collective-permute-start(bf16[256,1024]{1,0:T(8,128)(2,1)S(1)} %get-tuple-element.195.r0), channel_id=1, source_target_pairs={{0,1},{1,0},{2,3},{3,2},{4,5},{5,4},{6,7},{7,6},{8,9},{9,8},{10,11... | collective-permute-start | bytes 1572872 | tf_op jit(solution)/shard_map/ppermute | solution.py:269
  182.1 13.2 %collective-permute-start.36 = (bf16[256,1024]{1,0:T(8,128)(2,1)S(1)}, bf16[256,1024]{1,0:T(8,128)(2,1)S(1)}, u32[]{:S(2)}, u32[]{:S(2)}) collective-permute-start(bf16[256,1024]{1,0:T(8,128)(2,1)S(1)} %add_convert_fusion.1), channel_id=1, source_target_pairs={{0,1},{1,0},{2,3},{3,2},{4,5},{5,4},{6,7},{7,6},{8,9},{9,8},{10,11... | collective-permute-start | bytes 1572872 | tf_op jit(solution)/shard_map/ppermute | solution.py:269
  183.4 10.2 %collective-permute-start.35 = (bf16[256,1024]{1,0:T(8,128)(2,1)S(1)}, bf16[256,1024]{1,0:T(8,128)(2,1)S(1)}, u32[]{:S(2)}, u32[]{:S(2)}) collective-permute-start(bf16[256,1024]{1,0:T(8,128)(2,1)S(1)} %convolution_convert_fusion), channel_id=1, source_target_pairs={{0,16},{16,0},{1,17},{17,1},{2,18},{18,2},{3,19},{19,3},{4,20},{20... | collective-permute-start | bytes 1572872 | tf_op jit(solution)/shard_map/ppermute | solution.py:269
  188.0 24.9 %collective-permute-start.38 = (bf16[4,256,512]{2,1,0:T(8,128)(2,1)S(1)}, bf16[4,256,512]{2,1,0:T(8,128)(2,1)S(1)}, u32[]{:S(2)}, u32[]{:S(2)}) collective-permute-start(bf16[4,256,512]{2,1,0:T(8,128)(2,1)S(1)} %get-tuple-element.209), channel_id=1, source_target_pairs={{0,2},{2,0},{1,3},{3,1},{4,6},{6,4},{5,7},{7,5},{8,10},{10,8},{9,1... | collective-permute-start | bytes 3145736 | tf_op jit(solution)/shard_map/ppermute | solution.py:269
  196.9 16.0 %collective-permute-start.37 = (bf16[256,1024]{1,0:T(8,128)(2,1)S(1)}, bf16[256,1024]{1,0:T(8,128)(2,1)S(1)}, u32[]{:S(2)}, u32[]{:S(2)}) collective-permute-start(bf16[256,1024]{1,0:T(8,128)(2,1)S(1)} %get-tuple-element.206.d0), channel_id=1, source_target_pairs={{0,1},{1,0},{2,3},{3,2},{4,5},{5,4},{6,7},{7,6},{8,9},{9,8},{10,11... | collective-permute-start | bytes 1572872 | tf_op jit(solution)/shard_map/ppermute | solution.py:269
  215.5 24.8 %collective-permute-start.43 = (bf16[4,264,512]{2,1,0:T(8,128)(2,1)S(1)}, bf16[4,264,512]{2,1,0:T(8,128)(2,1)S(1)}, u32[]{:S(2)}, u32[]{:S(2)}) collective-permute-start(bf16[4,264,512]{2,1,0:T(8,128)(2,1)S(1)} %get-tuple-element.223), channel_id=1, source_target_pairs={{0,2},{2,0},{1,3},{3,1},{4,6},{6,4},{5,7},{7,5},{8,10},{10,8},{9,1... | collective-permute-start | bytes 3244040 | tf_op jit(solution)/shard_map/ppermute | solution.py:269
  220.5 23.4 %collective-permute-start.44 = (bf16[256,512]{1,0:T(8,128)(2,1)S(1)}, bf16[256,512]{1,0:T(8,128)(2,1)S(1)}, u32[]{:S(2)}, u32[]{:S(2)}) collective-permute-start(bf16[256,512]{1,0:T(8,128)(2,1)S(1)} %get-tuple-element.218), channel_id=1, source_target_pairs={{0,12},{4,0},{8,4},{12,8},{1,13},{5,1},{9,5},{13,9},{2,14},{6,2},{... | collective-permute-start | bytes 786440 | tf_op jit(solution)/shard_map/ppermute | solution.py:274
  222.4 23.4 %collective-permute-start.45 = (bf16[256,512]{1,0:T(8,128)(2,1)S(1)}, bf16[256,512]{1,0:T(8,128)(2,1)S(1)}, u32[]{:S(2)}, u32[]{:S(2)}) collective-permute-start(bf16[256,512]{1,0:T(8,128)(2,1)S(1)} %get-tuple-element.219), channel_id=1, source_target_pairs={{0,8},{4,12},{8,0},{12,4},{1,9},{5,13},{9,1},{13,5},{2,10},{6,14},... | collective-permute-start | bytes 786440 | tf_op jit(solution)/shard_map/ppermute | solution.py:274
  222.4 24.1 %collective-permute-start.46 = (bf16[256,512]{1,0:T(8,128)(2,1)S(1)}, bf16[256,512]{1,0:T(8,128)(2,1)S(1)}, u32[]{:S(2)}, u32[]{:S(2)}) collective-permute-start(bf16[256,512]{1,0:T(8,128)(2,1)S(1)} %get-tuple-element.220), channel_id=1, source_target_pairs={{0,4},{4,8},{8,12},{12,0},{1,5},{5,9},{9,13},{13,1},{2,6},{6,10},{... | collective-permute-start | bytes 786440 | tf_op jit(solution)/shard_map/ppermute | solution.py:274
  222.8 24.4 %collective-permute-start.41 = (bf16[2,256,256]{2,1,0:T(8,128)(2,1)S(1)}, bf16[2,256,256]{2,1,0:T(8,128)(2,1)S(1)}, u32[]{:S(2)}, u32[]{:S(2)}) collective-permute-start(bf16[2,256,256]{2,1,0:T(8,128)(2,1)S(1)} %pad_maximum_fusion.11), channel_id=1, source_target_pairs={{0,16},{16,0},{1,17},{17,1},{2,18},{18,2},{3,19},{19,3},{4,20},{20... | collective-permute-start | bytes 786440 | tf_op jit(solution)/shard_map/ppermute | solution.py:269
  240.2 21.0 %collective-permute-start.50 = (bf16[2,2,272,256]{3,2,1,0:T(8,128)(2,1)}, bf16[2,2,272,256]{3,2,1,0:T(8,128)(2,1)}, u32[]{:S(2)}, u32[]{:S(2)}) collective-permute-start(bf16[2,2,272,256]{3,2,1,0:T(8,128)(2,1)} %get-tuple-element.229), channel_id=1, source_target_pairs={{0,2},{2,0},{1,3},{3,1},{4,6},{6,4},{5,7},{7,5},{8,10},{10,8},{9,1... | collective-permute-start | bytes 1671176 | tf_op jit(solution)/shard_map/ppermute | solution.py:269
  243.9 14.2 %collective-permute-start.47 = (bf16[264,512]{1,0:T(8,128)(2,1)S(1)}, bf16[264,512]{1,0:T(8,128)(2,1)S(1)}, u32[]{:S(2)}, u32[]{:S(2)}) collective-permute-start(bf16[264,512]{1,0:T(8,128)(2,1)S(1)} %get-tuple-element.231), channel_id=1, source_target_pairs={{0,12},{4,0},{8,4},{12,8},{1,13},{5,1},{9,5},{13,9},{2,14},{6,2},{... | collective-permute-start | bytes 811016 | tf_op jit(solution)/shard_map/ppermute | solution.py:274
  246.5 11.6 %collective-permute-start.48 = (bf16[264,512]{1,0:T(8,128)(2,1)S(1)}, bf16[264,512]{1,0:T(8,128)(2,1)S(1)}, u32[]{:S(2)}, u32[]{:S(2)}) collective-permute-start(bf16[264,512]{1,0:T(8,128)(2,1)S(1)} %get-tuple-element.233), channel_id=1, source_target_pairs={{0,4},{4,8},{8,12},{12,0},{1,5},{5,9},{9,13},{13,1},{2,6},{6,10},{... | collective-permute-start | bytes 811016 | tf_op jit(solution)/shard_map/ppermute | solution.py:274
  258.8 14.5 %collective-permute-start.49 = (bf16[2,2,272,256]{3,2,1,0:T(8,128)(2,1)}, bf16[2,2,272,256]{3,2,1,0:T(8,128)(2,1)}, u32[]{:S(2)}, u32[]{:S(2)}) collective-permute-start(bf16[2,2,272,256]{3,2,1,0:T(8,128)(2,1)} %get-tuple-element.237), channel_id=1, source_target_pairs={{0,2},{2,0},{1,3},{3,1},{4,6},{6,4},{5,7},{7,5},{8,10},{10,8},{9,1... | collective-permute-start | bytes 1671176 | tf_op jit(solution)/shard_map/ppermute | solution.py:269
  258.8 14.4 %collective-permute-start.51 = (bf16[264,512]{1,0:T(8,128)(2,1)}, bf16[264,512]{1,0:T(8,128)(2,1)}, u32[]{:S(2)}, u32[]{:S(2)}) collective-permute-start(bf16[264,512]{1,0:T(8,128)(2,1)} %get-tuple-element.232), channel_id=1, source_target_pairs={{0,8},{4,12},{8,0},{12,4},{1,9},{5,13},{9,1},{13,5},{2,10},{6,14},... | collective-permute-start | bytes 811016 | tf_op jit(solution)/shard_map/ppermute | solution.py:274
  275.9 7.7 %collective-permute-start.53 = (bf16[256,1024]{1,0:T(8,128)(2,1)S(1)}, bf16[256,1024]{1,0:T(8,128)(2,1)S(1)}, u32[]{:S(2)}, u32[]{:S(2)}) collective-permute-start(bf16[256,1024]{1,0:T(8,128)(2,1)S(1)} %fusion.16), channel_id=1, source_target_pairs={{0,16},{16,0},{1,17},{17,1},{2,18},{18,2},{3,19},{19,3},{4,20},{20... | collective-permute-start | bytes 1572872 | tf_op jit(solution)/shard_map/ppermute | solution.py:269
  278.1 15.4 %collective-permute-start.56 = (bf16[2,272,256]{2,1,0:T(8,128)(2,1)S(1)}, bf16[2,272,256]{2,1,0:T(8,128)(2,1)S(1)}, u32[]{:S(2)}, u32[]{:S(2)}) collective-permute-start(bf16[2,272,256]{2,1,0:T(8,128)(2,1)S(1)} %get-tuple-element.240), channel_id=1, source_target_pairs={{0,12},{4,0},{8,4},{12,8},{1,13},{5,1},{9,5},{13,9},{2,14},{6,2},{... | collective-permute-start | bytes 835592 | tf_op jit(solution)/shard_map/ppermute | solution.py:274
  280.8 10.8 %collective-permute-start.52 = (bf16[256,1024]{1,0:T(8,128)(2,1)S(1)}, bf16[256,1024]{1,0:T(8,128)(2,1)S(1)}, u32[]{:S(2)}, u32[]{:S(2)}) collective-permute-start(bf16[256,1024]{1,0:T(8,128)(2,1)S(1)} %pad_maximum_fusion.6), channel_id=1, source_target_pairs={{0,0},{2,16},{16,2},{18,18},{1,1},{3,17},{17,3},{19,19},{4,4},{6,2... | collective-permute-start | bytes 1572872 | tf_op jit(solution)/shard_map/ppermute | solution.py:1053
  284.0 24.2 %collective-permute-start.55 = (bf16[256,1024]{1,0:T(8,128)(2,1)S(1)}, bf16[256,1024]{1,0:T(8,128)(2,1)S(1)}, u32[]{:S(2)}, u32[]{:S(2)}) collective-permute-start(bf16[256,1024]{1,0:T(8,128)(2,1)S(1)} %fusion.15), channel_id=1, source_target_pairs={{0,1},{1,0},{2,3},{3,2},{4,5},{5,4},{6,7},{7,6},{8,9},{9,8},{10,11... | collective-permute-start | bytes 1572872 | tf_op jit(solution)/shard_map/ppermute | solution.py:269
  287.4 20.9 %collective-permute-start.54 = (bf16[256,1024]{1,0:T(8,128)(2,1)S(1)}, bf16[256,1024]{1,0:T(8,128)(2,1)S(1)}, u32[]{:S(2)}, u32[]{:S(2)}) collective-permute-start(bf16[256,1024]{1,0:T(8,128)(2,1)S(1)} %get-tuple-element.257), channel_id=1, source_target_pairs={{0,16},{16,0},{1,17},{17,1},{2,18},{18,2},{3,19},{19,3},{4,20},{20... | collective-permute-start | bytes 1572872 | tf_op jit(solution)/shard_map/ppermute | solution.py:269
  287.4 20.8 %collective-permute-start.57 = (bf16[2,272,256]{2,1,0:T(8,128)(2,1)S(1)}, bf16[2,272,256]{2,1,0:T(8,128)(2,1)S(1)}, u32[]{:S(2)}, u32[]{:S(2)}) collective-permute-start(bf16[2,272,256]{2,1,0:T(8,128)(2,1)S(1)} %get-tuple-element.241), channel_id=1, source_target_pairs={{0,8},{4,12},{8,0},{12,4},{1,9},{5,13},{9,1},{13,5},{2,10},{6,14},... | collective-permute-start | bytes 835592 | tf_op jit(solution)/shard_map/ppermute | solution.py:274
  291.6 16.7 %collective-permute-start.58 = (bf16[2,272,256]{2,1,0:T(8,128)(2,1)S(1)}, bf16[2,272,256]{2,1,0:T(8,128)(2,1)S(1)}, u32[]{:S(2)}, u32[]{:S(2)}) collective-permute-start(bf16[2,272,256]{2,1,0:T(8,128)(2,1)S(1)} %get-tuple-element.242), channel_id=1, source_target_pairs={{0,4},{4,8},{8,12},{12,0},{1,5},{5,9},{9,13},{13,1},{2,6},{6,10},{... | collective-permute-start | bytes 835592 | tf_op jit(solution)/shard_map/ppermute | solution.py:274
  293.4 14.8 %collective-permute-start.59 = (bf16[520,256]{1,0:T(8,128)(2,1)S(1)}, bf16[520,256]{1,0:T(8,128)(2,1)S(1)}, u32[]{:S(2)}, u32[]{:S(2)}) collective-permute-start(bf16[520,256]{1,0:T(8,128)(2,1)S(1)} %get-tuple-element.261), channel_id=1, source_target_pairs={{0,1},{1,0},{2,3},{3,2},{4,5},{5,4},{6,7},{7,6},{8,9},{9,8},{10,11... | collective-permute-start | bytes 798728 | tf_op jit(solution)/shard_map/ppermute | solution.py:269
  309.6 10.5 %collective-permute-start.60 = (bf16[256,1024]{1,0:T(8,128)(2,1)S(1)}, bf16[256,1024]{1,0:T(8,128)(2,1)S(1)}, u32[]{:S(2)}, u32[]{:S(2)}) collective-permute-start(bf16[256,1024]{1,0:T(8,128)(2,1)S(1)} %add_convert_fusion), channel_id=1, source_target_pairs={{0,0},{2,16},{16,2},{18,18},{1,1},{3,17},{17,3},{19,19},{4,4},{6,2... | collective-permute-start | bytes 1572872 | tf_op jit(solution)/shard_map/ppermute | solution.py:1067
  (86 other events, 951.4 us)
